TPU v7x, 512 devices: a whole 4x8x8 slice. The times are simulated.
512 devices in a mesh: gx: 16 (over x_lo, y), gy: 32 (over x_hi, z, core).
Axes of the slice: x: 4 (x_hi: 2, x_lo: 2; x = x_hi * 2 + x_lo), y: 8, z: 8, core: 2. Of those that a mesh axis runs over, the one named last changes fastest.
Arguments:
- fluid_pops: float32 [19, 2, 256, 4096], P(None, None, 'gx', 'gy'), may hold values from 0.01 to 0.6, as said below
- magnet_pops: float32 [3, 7, 2, 256, 4096], P(None, None, None, 'gx', 'gy'), may hold values from -0.12 to 0.12
Outputs:
- fluid_next: float32 [19, 2, 256, 4096], P(None, None, 'gx', 'gy')
- magnet_next: float32 [3, 7, 2, 256, 4096], P(None, None, None, 'gx', 'gy')
Inputs may be any that keep to these rules, and one draw needn't show every extreme that they name: `fluid_pops`: every fluid population is positive.
All inputs are finite; a program needn't handle non-finite values.
Results may differ from a plain program's by a relative error of at most 0.0001.
Values sent between devices are 32-bit elements; how exact they have to be, the bound alone decides.
A program may use at most 64 MiB of HBM per device.

v0:
```python
import jax
import jax.numpy as jnp
import numpy as np
from jax import lax
from jax.sharding import PartitionSpec as P

STEPS = 2


FLUID_VELOCITY = np.array(
    [
        [0, 0, 0],
        [1, 0, 0],
        [-1, 0, 0],
        [0, 1, 0],
        [0, -1, 0],
        [0, 0, 1],
        [0, 0, -1],
        [1, 1, 0],
        [-1, -1, 0],
        [1, -1, 0],
        [-1, 1, 0],
        [1, 0, 1],
        [-1, 0, -1],
        [1, 0, -1],
        [-1, 0, 1],
        [0, 1, 1],
        [0, -1, -1],
        [0, 1, -1],
        [0, -1, 1],
    ]
)
FLUID_WEIGHT = [1.0 / 3.0] + [1.0 / 18.0] * 6 + [1.0 / 36.0] * 12
MAGNET_WEIGHT = [0.25] + [0.125] * 6
TAU_FLUID = 0.9
TAU_MAGNET = 0.8
ALL_VELOCITY = [FLUID_VELOCITY[index] for index in range(19)] + [
    FLUID_VELOCITY[index] for comp in range(3) for index in range(7)
]


def extended(array, sides, width):
    for axis, dim in sides:
        devices, length = (lax.axis_size(axis), array.shape[dim])
        up = [(i, (i + 1) % devices) for i in range(devices)]
        down = [(j, i) for i, j in up]
        last = lax.slice_in_dim(array, length - width, length, axis=dim)
        leading = lax.slice_in_dim(array, 0, width, axis=dim)
        before = lax.ppermute(last, axis, up)
        after = lax.ppermute(leading, axis, down)
        array = jnp.concatenate([before, array, after], axis=dim)
    return array


def collide(fluid_pops, magnet_pops):
    density = jnp.sum(fluid_pops, axis=0)
    velocity = []
    for comp in range(3):
        moment = jnp.zeros_like(density)
        for index in range(19):
            if FLUID_VELOCITY[index, comp] != 0:
                moment = moment + float(FLUID_VELOCITY[index, comp]) * fluid_pops[index]
        velocity.append(moment / density)
    induction = [jnp.sum(magnet_pops[comp], axis=0) for comp in range(3)]
    field_sq = (
        induction[0] * induction[0] + induction[1] * induction[1] + induction[2] * induction[2]
    )
    stress = [
        [
            density * velocity[one] * velocity[two]
            - induction[one] * induction[two]
            + (0.5 * field_sq if one == two else 0.0)
            for two in range(3)
        ]
        for one in range(3)
    ]
    stress_trace = stress[0][0] + stress[1][1] + stress[2][2]
    fluid_post = []
    for index in range(19):
        speed = jnp.zeros_like(density)
        contract = jnp.zeros_like(density)
        for one in range(3):
            if FLUID_VELOCITY[index, one] != 0:
                speed = speed + float(FLUID_VELOCITY[index, one]) * velocity[one]
                for two in range(3):
                    if FLUID_VELOCITY[index, two] != 0:
                        contract = (
                            contract
                            + float(FLUID_VELOCITY[index, one] * FLUID_VELOCITY[index, two])
                            * stress[one][two]
                        )
        balance = FLUID_WEIGHT[index] * (
            density + 3.0 * density * speed + 4.5 * (contract - stress_trace / 3.0)
        )
        fluid_post.append(fluid_pops[index] - (fluid_pops[index] - balance) / TAU_FLUID)
    magnet_post = []
    for comp in range(3):
        for index in range(7):
            flux = jnp.zeros_like(density)
            for other in range(3):
                if FLUID_VELOCITY[index, other] != 0:
                    flux = flux + float(FLUID_VELOCITY[index, other]) * (
                        velocity[other] * induction[comp] - induction[other] * velocity[comp]
                    )
            balance = MAGNET_WEIGHT[index] * (induction[comp] + 4.0 * flux)
            magnet_post.append(
                magnet_pops[comp, index] - (magnet_pops[comp, index] - balance) / TAU_MAGNET
            )
    return jnp.stack(fluid_post + magnet_post)


def collide_stack(populations):
    magnet_part = populations[19:].reshape((3, 7) + populations.shape[1:])
    return collide(populations[:19], magnet_part)


def stream_inner(padded):
    extent_x = padded.shape[2] - 2
    extent_y = padded.shape[3] - 2
    pieces = []
    for index in range(40):
        step_x, step_y, step_z = (int(v) for v in ALL_VELOCITY[index])
        shifted = padded[
            index, :, 1 - step_x : 1 - step_x + extent_x, 1 - step_y : 1 - step_y + extent_y
        ]
        if step_z != 0:
            shifted = jnp.roll(shifted, step_z, axis=0)
        pieces.append(shifted)
    return jnp.stack(pieces)


def extend(populations, width):
    return extended(populations, (("gx", 2), ("gy", 3)), width)


def per_device(fluid_pops, magnet_pops):
    populations = jnp.concatenate(
        [fluid_pops, magnet_pops.reshape((21,) + magnet_pops.shape[2:])], axis=0
    )
    for step_index in range(STEPS):
        populations = stream_inner(extend(collide_stack(populations), 1))
    return (populations[:19], populations[19:].reshape(magnet_pops.shape))


def solution(mesh):
    return jax.shard_map(
        per_device,
        mesh=mesh,
        in_specs=(P(None, None, "gx", "gy"), P(None, None, None, "gx", "gy")),
        out_specs=(P(None, None, "gx", "gy"), P(None, None, None, "gx", "gy")),
        check_vma=False,
    )
```

profile of v0, /device:TPU:24, one launch (start us, length us, event | category | flops | bytes accessed | tf_op | source)
XLA Modules:
  0.0 88.0 jit_solution(13906325334503174046)
XLA Ops:
  0.6 1.1 %slice_reduce_fusion.2 = (f32[2,16,128]{2,1,0:T(8,128)S(1)}, f32[2,16,128]{2,1,0:T(8,128)S(1)}, f32[2,16,128]{2,1,0:T(8,128)S(1)}) fusion(f32[3,7,2,16,128]{4,3,2,1,0:T(8,128)} %param.3), kind=kLoop, calls=%fused_computation.145 | loop fusion | flops 73728 | bytes 393216 | tf_op jit(solution)/shard_map/reduce_sum | solution.py:64
  4.2 4.7 %collective-permute-start = (f32[40,2,1,128]{3,2,1,0:T(1,128)S(1)}, f32[40,2,1,128]{3,2,1,0:T(1,128)S(1)}, u32[]{:S(2)}, u32[]{:S(2)}) collective-permute-start(f32[40,2,1,128]{3,2,1,0:T(1,128)S(1)} %get-tuple-element.144), channel_id=1, source_target_pairs={{0,32},{32,64},{64,96},{96,128},{128,160},{160,192},{192,224},{224... | collective-permute-start | bytes 122888 | tf_op jit(solution)/shard_map/ppermute | solution.py:49
  8.9 1.9 %collective-permute-start.1 = (f32[40,2,1,128]{3,2,1,0:T(1,128)S(1)}, f32[40,2,1,128]{3,2,1,0:T(1,128)S(1)}, u32[]{:S(2)}, u32[]{:S(2)}) collective-permute-start(f32[40,2,1,128]{3,2,1,0:T(1,128)S(1)} %get-tuple-element.143), channel_id=1, source_target_pairs={{32,0},{64,32},{96,64},{128,96},{160,128},{192,160},{224,192},{256... | collective-permute-start | bytes 122888 | tf_op jit(solution)/shard_map/ppermute | solution.py:50
  14.0 2.0 %collective-permute-done.1 = f32[40,2,1,128]{3,2,1,0:T(1,128)S(1)} collective-permute-done((f32[40,2,1,128]{3,2,1,0:T(1,128)S(1)}, f32[40,2,1,128]{3,2,1,0:T(1,128)S(1)}, u32[]{:S(2)}, u32[]{:S(2)}) %collective-permute-start.1) | collective-permute-done | bytes 40992 | tf_op jit(solution)/shard_map/ppermute | solution.py:50
  16.5 1.0 %copy.128 = f32[40,2,18,1]{0,1,3,2:T(2,128)} copy(f32[40,2,18,1]{3,2,1,0:T(8,128)S(1)} %get-tuple-element.116) | data formatting | bytes 11520 | tf_op jit(solution)/shard_map/slice | solution.py:47
  17.4 1.9 %collective-permute-start.2 = (f32[40,2,18,1]{0,1,3,2:T(2,128)}, f32[40,2,18,1]{0,1,3,2:T(2,128)S(1)}, u32[]{:S(2)}, u32[]{:S(2)}) collective-permute-start(f32[40,2,18,1]{0,1,3,2:T(2,128)} %copy.128), channel_id=1, source_target_pairs={{0,1},{1,2},{2,3},{3,4},{4,5},{5,6},{6,7},{7,8},{8,9},{9,10},{10,1... | collective-permute-start | bytes 17288 | tf_op jit(solution)/shard_map/ppermute | solution.py:49
  19.7 11.4 %collective-permute-start.3 = (f32[40,2,18,1]{0,1,3,2:T(2,128)S(1)}, f32[40,2,18,1]{0,1,3,2:T(2,128)}, u32[]{:S(2)}, u32[]{:S(2)}) collective-permute-start(f32[40,2,18,1]{0,1,3,2:T(2,128)S(1)} %copy.130), channel_id=1, source_target_pairs={{1,0},{2,1},{3,2},{4,3},{5,4},{6,5},{7,6},{8,7},{9,8},{10,9},{11,1... | collective-permute-start | bytes 17288 | tf_op jit(solution)/shard_map/ppermute | solution.py:50
  32.9 1.2 %copy.131 = f32[40,2,18,1]{3,2,1,0:T(8,128)S(1)} copy(f32[40,2,18,1]{0,1,3,2:T(2,128)} %collective-permute-done.3) | data formatting | bytes 11520 | tf_op jit(solution)/shard_map/ppermute | solution.py:50
  43.7 0.7 constant_dynamic-update-slice_fusion.42
  45.8 0.8 copy-done.2
  50.2 4.0 %collective-permute-start.4 = (f32[40,2,1,128]{3,2,1,0:T(1,128)S(1)}, f32[40,2,1,128]{3,2,1,0:T(1,128)S(1)}, u32[]{:S(2)}, u32[]{:S(2)}) collective-permute-start(f32[40,2,1,128]{3,2,1,0:T(1,128)S(1)} %get-tuple-element.140), channel_id=1, source_target_pairs={{0,32},{32,64},{64,96},{96,128},{128,160},{160,192},{192,224},{224... | collective-permute-start | bytes 122888 | tf_op jit(solution)/shard_map/ppermute | solution.py:49
  54.2 1.9 %collective-permute-start.5 = (f32[40,2,1,128]{3,2,1,0:T(1,128)S(1)}, f32[40,2,1,128]{3,2,1,0:T(1,128)S(1)}, u32[]{:S(2)}, u32[]{:S(2)}) collective-permute-start(f32[40,2,1,128]{3,2,1,0:T(1,128)S(1)} %get-tuple-element.139), channel_id=1, source_target_pairs={{32,0},{64,32},{96,64},{128,96},{160,128},{192,160},{224,192},{256... | collective-permute-start | bytes 122888 | tf_op jit(solution)/shard_map/ppermute | solution.py:50
  56.2 5.1 %collective-permute-done.5 = f32[40,2,1,128]{3,2,1,0:T(1,128)S(1)} collective-permute-done((f32[40,2,1,128]{3,2,1,0:T(1,128)S(1)}, f32[40,2,1,128]{3,2,1,0:T(1,128)S(1)}, u32[]{:S(2)}, u32[]{:S(2)}) %collective-permute-start.5) | collective-permute-done | bytes 40992 | tf_op jit(solution)/shard_map/ppermute | solution.py:50
  62.2 1.9 %collective-permute-start.6 = (f32[40,2,18,1]{0,1,3,2:T(2,128)S(1)}, f32[40,2,18,1]{0,1,3,2:T(2,128)S(1)}, u32[]{:S(2)}, u32[]{:S(2)}) collective-permute-start(f32[40,2,18,1]{0,1,3,2:T(2,128)S(1)} %copy.132), channel_id=1, source_target_pairs={{0,1},{1,2},{2,3},{3,4},{4,5},{5,6},{6,7},{7,8},{8,9},{9,10},{10,1... | collective-permute-start | bytes 17288 | tf_op jit(solution)/shard_map/ppermute | solution.py:49
  64.5 7.2 %collective-permute-start.7 = (f32[40,2,18,1]{0,1,3,2:T(2,128)S(1)}, f32[40,2,18,1]{0,1,3,2:T(2,128)S(1)}, u32[]{:S(2)}, u32[]{:S(2)}) collective-permute-start(f32[40,2,18,1]{0,1,3,2:T(2,128)S(1)} %copy.134), channel_id=1, source_target_pairs={{1,0},{2,1},{3,2},{4,3},{5,4},{6,5},{7,6},{8,7},{9,8},{10,9},{11,1... | collective-permute-start | bytes 17288 | tf_op jit(solution)/shard_map/ppermute | solution.py:50
  74.0 0.7 constant_dynamic-update-slice_fusion.137
  74.7 0.7 constant_dynamic-update-slice_fusion.136
  76.6 1.3 %constant_dynamic-update-slice_fusion.133 = f32[21,2,16,128]{3,2,1,0:T(8,128)} fusion(f32[21,2,16,128]{3,2,1,0:T(8,128)} %constant_dynamic-update-slice_fusion.134, f32[1,2,16,128]{3,2,1,0:T(8,128)S(1)} %get-tuple-element.64, f32[3,7,2,16,128]{4,3,2,1,0:T(8,128)} %bitcast.1540), kind=kLoop, calls=%fused_computation.135 | loop fusion | flops 16384 | bytes 49152
  79.1 0.7 constant_dynamic-update-slice_fusion.130
  79.8 0.7 constant_dynamic-update-slice_fusion.129
  81.7 1.3 %constant_dynamic-update-slice_fusion.126 = f32[21,2,16,128]{3,2,1,0:T(8,128)} fusion(f32[21,2,16,128]{3,2,1,0:T(8,128)} %constant_dynamic-update-slice_fusion.127, f32[1,2,16,128]{3,2,1,0:T(8,128)S(1)} %get-tuple-element.65, f32[3,7,2,16,128]{4,3,2,1,0:T(8,128)} %bitcast.1541), kind=kLoop, calls=%fused_computation.128 | loop fusion | flops 16384 | bytes 49152
  84.3 0.7 constant_dynamic-update-slice_fusion.123
  85.1 0.7 constant_dynamic-update-slice_fusion.122
  87.3 0.7 copy-done.36
  (242 shorter events, 32.0 us)
Async XLA Ops:
  0.6 1.1 %copy-start = (f32[19,2,16,128]{3,2,1,0:T(8,128)S(1)}, f32[19,2,16,128]{3,2,1,0:T(8,128)}, u32[]{:S(2)}) copy-start(f32[19,2,16,128]{3,2,1,0:T(8,128)} %param.2) | copy-start | bytes 933892
  0.6 1.2 %copy-start.1 = (f32[3,7,2,16,128]{4,3,2,1,0:T(8,128)S(1)}, f32[3,7,2,16,128]{4,3,2,1,0:T(8,128)}, u32[]{:S(2)}) copy-start(f32[3,7,2,16,128]{4,3,2,1,0:T(8,128)} %param.3) | copy-start | bytes 1032196
  4.2 9.8 %collective-permute-start = (f32[40,2,1,128]{3,2,1,0:T(1,128)S(1)}, f32[40,2,1,128]{3,2,1,0:T(1,128)S(1)}, u32[]{:S(2)}, u32[]{:S(2)}) collective-permute-start(f32[40,2,1,128]{3,2,1,0:T(1,128)S(1)} %get-tuple-element.144), channel_id=1, source_target_pairs={{0,32},{32,64},{64,96},{96,128},{128,160},{160,192},{192,224},{224... | collective-permute-start | bytes 122888 | tf_op jit(solution)/shard_map/ppermute | solution.py:49
  8.9 7.1 %collective-permute-start.1 = (f32[40,2,1,128]{3,2,1,0:T(1,128)S(1)}, f32[40,2,1,128]{3,2,1,0:T(1,128)S(1)}, u32[]{:S(2)}, u32[]{:S(2)}) collective-permute-start(f32[40,2,1,128]{3,2,1,0:T(1,128)S(1)} %get-tuple-element.143), channel_id=1, source_target_pairs={{32,0},{64,32},{96,64},{128,96},{160,128},{192,160},{224,192},{256... | collective-permute-start | bytes 122888 | tf_op jit(solution)/shard_map/ppermute | solution.py:50
  17.4 15.0 %collective-permute-start.2 = (f32[40,2,18,1]{0,1,3,2:T(2,128)}, f32[40,2,18,1]{0,1,3,2:T(2,128)S(1)}, u32[]{:S(2)}, u32[]{:S(2)}) collective-permute-start(f32[40,2,18,1]{0,1,3,2:T(2,128)} %copy.128), channel_id=1, source_target_pairs={{0,1},{1,2},{2,3},{3,4},{4,5},{5,6},{6,7},{7,8},{8,9},{9,10},{10,1... | collective-permute-start | bytes 17288 | tf_op jit(solution)/shard_map/ppermute | solution.py:49
  19.7 13.2 %collective-permute-start.3 = (f32[40,2,18,1]{0,1,3,2:T(2,128)S(1)}, f32[40,2,18,1]{0,1,3,2:T(2,128)}, u32[]{:S(2)}, u32[]{:S(2)}) collective-permute-start(f32[40,2,18,1]{0,1,3,2:T(2,128)S(1)} %copy.130), channel_id=1, source_target_pairs={{1,0},{2,1},{3,2},{4,3},{5,4},{6,5},{7,6},{8,7},{9,8},{10,9},{11,1... | collective-permute-start | bytes 17288 | tf_op jit(solution)/shard_map/ppermute | solution.py:50
  39.3 1.3 %copy-start.21 = (f32[1,16,128]{2,1,0:T(8,128)S(1)}, f32[1,16,128]{2,1,0:T(8,128)}, u32[]{:S(2)}) copy-start(f32[1,16,128]{2,1,0:T(8,128)} %get-tuple-element.201) | copy-start | bytes 24580
  39.3 1.3 %copy-start.22 = (f32[1,16,128]{2,1,0:T(8,128)S(1)}, f32[1,16,128]{2,1,0:T(8,128)}, u32[]{:S(2)}) copy-start(f32[1,16,128]{2,1,0:T(8,128)} %get-tuple-element.202) | copy-start | bytes 24580
  43.7 1.3 %copy-start.11 = (f32[1,16,128]{2,1,0:T(8,128)S(1)}, f32[1,16,128]{2,1,0:T(8,128)}, u32[]{:S(2)}) copy-start(f32[1,16,128]{2,1,0:T(8,128)} %get-tuple-element.193) | copy-start | bytes 24580
  43.7 1.3 %copy-start.12 = (f32[1,16,128]{2,1,0:T(8,128)S(1)}, f32[1,16,128]{2,1,0:T(8,128)}, u32[]{:S(2)}) copy-start(f32[1,16,128]{2,1,0:T(8,128)} %get-tuple-element.194) | copy-start | bytes 24580
  45.7 1.0 %copy-start.2 = (f32[21,2,16,128]{3,2,1,0:T(8,128)S(1)}, f32[21,2,16,128]{3,2,1,0:T(8,128)}, u32[]{:S(2)}) copy-start(f32[21,2,16,128]{3,2,1,0:T(8,128)} %constant_dynamic-update-slice_fusion.40) | copy-start | bytes 1032196
  47.1 1.3 %copy-start.10 = (f32[1,1,16,128]{3,2,1,0:T(8,128)S(1)}, f32[1,1,16,128]{3,2,1,0:T(8,128)}, u32[]{:S(2)}) copy-start(f32[1,1,16,128]{3,2,1,0:T(8,128)} %get-tuple-element.222) | copy-start | bytes 24580
  47.1 1.3 %copy-start.24 = (f32[1,1,16,128]{3,2,1,0:T(8,128)S(1)}, f32[1,1,16,128]{3,2,1,0:T(8,128)}, u32[]{:S(2)}) copy-start(f32[1,1,16,128]{3,2,1,0:T(8,128)} %get-tuple-element.195) | copy-start | bytes 24580
  47.1 1.3 %copy-start.25 = (f32[1,1,16,128]{3,2,1,0:T(8,128)S(1)}, f32[1,1,16,128]{3,2,1,0:T(8,128)}, u32[]{:S(2)}) copy-start(f32[1,1,16,128]{3,2,1,0:T(8,128)} %get-tuple-element.196) | copy-start | bytes 24580
  47.1 1.3 %copy-start.26 = (f32[1,1,16,128]{3,2,1,0:T(8,128)S(1)}, f32[1,1,16,128]{3,2,1,0:T(8,128)}, u32[]{:S(2)}) copy-start(f32[1,1,16,128]{3,2,1,0:T(8,128)} %get-tuple-element.191) | copy-start | bytes 24580
  47.1 1.3 %copy-start.27 = (f32[1,1,16,128]{3,2,1,0:T(8,128)S(1)}, f32[1,1,16,128]{3,2,1,0:T(8,128)}, u32[]{:S(2)}) copy-start(f32[1,1,16,128]{3,2,1,0:T(8,128)} %get-tuple-element.192) | copy-start | bytes 24580
  47.1 1.3 %copy-start.28 = (f32[1,1,16,128]{3,2,1,0:T(8,128)S(1)}, f32[1,1,16,128]{3,2,1,0:T(8,128)}, u32[]{:S(2)}) copy-start(f32[1,1,16,128]{3,2,1,0:T(8,128)} %get-tuple-element.213) | copy-start | bytes 24580
  47.1 1.3 %copy-start.29 = (f32[1,1,16,128]{3,2,1,0:T(8,128)S(1)}, f32[1,1,16,128]{3,2,1,0:T(8,128)}, u32[]{:S(2)}) copy-start(f32[1,1,16,128]{3,2,1,0:T(8,128)} %get-tuple-element.214) | copy-start | bytes 24580
  47.1 1.3 %copy-start.30 = (f32[1,1,16,128]{3,2,1,0:T(8,128)S(1)}, f32[1,1,16,128]{3,2,1,0:T(8,128)}, u32[]{:S(2)}) copy-start(f32[1,1,16,128]{3,2,1,0:T(8,128)} %get-tuple-element.199) | copy-start | bytes 24580
  47.2 1.3 %copy-start.31 = (f32[1,1,16,128]{3,2,1,0:T(8,128)S(1)}, f32[1,1,16,128]{3,2,1,0:T(8,128)}, u32[]{:S(2)}) copy-start(f32[1,1,16,128]{3,2,1,0:T(8,128)} %get-tuple-element.200) | copy-start | bytes 24580
  50.2 6.0 %collective-permute-start.4 = (f32[40,2,1,128]{3,2,1,0:T(1,128)S(1)}, f32[40,2,1,128]{3,2,1,0:T(1,128)S(1)}, u32[]{:S(2)}, u32[]{:S(2)}) collective-permute-start(f32[40,2,1,128]{3,2,1,0:T(1,128)S(1)} %get-tuple-element.140), channel_id=1, source_target_pairs={{0,32},{32,64},{64,96},{96,128},{128,160},{160,192},{192,224},{224... | collective-permute-start | bytes 122888 | tf_op jit(solution)/shard_map/ppermute | solution.py:49
  54.2 7.1 %collective-permute-start.5 = (f32[40,2,1,128]{3,2,1,0:T(1,128)S(1)}, f32[40,2,1,128]{3,2,1,0:T(1,128)S(1)}, u32[]{:S(2)}, u32[]{:S(2)}) collective-permute-start(f32[40,2,1,128]{3,2,1,0:T(1,128)S(1)} %get-tuple-element.139), channel_id=1, source_target_pairs={{32,0},{64,32},{96,64},{128,96},{160,128},{192,160},{224,192},{256... | collective-permute-start | bytes 122888 | tf_op jit(solution)/shard_map/ppermute | solution.py:50
  62.2 10.8 %collective-permute-start.6 = (f32[40,2,18,1]{0,1,3,2:T(2,128)S(1)}, f32[40,2,18,1]{0,1,3,2:T(2,128)S(1)}, u32[]{:S(2)}, u32[]{:S(2)}) collective-permute-start(f32[40,2,18,1]{0,1,3,2:T(2,128)S(1)} %copy.132), channel_id=1, source_target_pairs={{0,1},{1,2},{2,3},{3,4},{4,5},{5,6},{6,7},{7,8},{8,9},{9,10},{10,1... | collective-permute-start | bytes 17288 | tf_op jit(solution)/shard_map/ppermute | solution.py:49
  64.5 9.0 %collective-permute-start.7 = (f32[40,2,18,1]{0,1,3,2:T(2,128)S(1)}, f32[40,2,18,1]{0,1,3,2:T(2,128)S(1)}, u32[]{:S(2)}, u32[]{:S(2)}) collective-permute-start(f32[40,2,18,1]{0,1,3,2:T(2,128)S(1)} %copy.134), channel_id=1, source_target_pairs={{1,0},{2,1},{3,2},{4,3},{5,4},{6,5},{7,6},{8,7},{9,8},{10,9},{11,1... | collective-permute-start | bytes 17288 | tf_op jit(solution)/shard_map/ppermute | solution.py:50
  (21 other events, 15.6 us)
where the time goes:
time: 88.9 us; the launch traced here: 88 us
  starting transfers between devices  35 us (39%)
  other arithmetic  32.5 us (37%)
  local copies, waits for them, and re-layouts  11.8 us (13%)
  waiting for transfers between devices  7.09 us (8%)
  between operations  1.63 us (2%)
    unnamed x128, other arithmetic  29 us
    ppermute x4, starting transfers between devices, extended(): after = lax.ppermute(leading, axis, down)  22.5 us
    ppermute x4, starting transfers between devices, extended(): before = lax.ppermute(last, axis, up)  12.5 us
    ppermute x4, waiting for transfers between devices, extended(): after = lax.ppermute(leading, axis, down)  7.08 us
    concatenate x5, local copies, waits for them, and re-layouts, stream_inner(): shifted = jnp.roll(shifted, step_z, axis=0)  3.14 us
    unnamed x75, local copies, waits for them, and re-layouts  3.08 us
  transfers between devices with their start and end apart: 8, of which 2 were waited for; matrix products, arithmetic and copies ran while one was open for 8% of the time, Pallas kernels for 0%

commit v1 on v0

v1 whole, which is shorter than its diff:
```python
import functools

import jax
import jax.numpy as jnp
from jax import lax
from jax.experimental import pallas as pl
from jax.experimental.pallas import tpu as pltpu
from jax.sharding import PartitionSpec as P

MESH = pl.DeviceIdType.MESH
F32 = jnp.float32

FLUID = [
    (0, 0, 0),
    (1, 0, 0), (-1, 0, 0), (0, 1, 0), (0, -1, 0), (0, 0, 1), (0, 0, -1),
    (1, 1, 0), (-1, -1, 0), (1, -1, 0), (-1, 1, 0),
    (1, 0, 1), (-1, 0, -1), (1, 0, -1), (-1, 0, 1),
    (0, 1, 1), (0, -1, -1), (0, 1, -1), (0, -1, 1),
]
VEL = FLUID + FLUID[:7] * 3
NPOP = 40
OM_F = 1.0 / 0.9
OM_G = 1.0 / 0.8

XP = [p for p in range(NPOP) if VEL[p][0] == 1]
X0 = [p for p in range(NPOP) if VEL[p][0] == 0]
XM = [p for p in range(NPOP) if VEL[p][0] == -1]
ORDER = XP + X0 + XM
POS = {p: i for i, p in enumerate(ORDER)}
XOFF = {}
for i, p in enumerate(XP):
    XOFF[p] = i
for i, p in enumerate(X0):
    XOFF[p] = 8 + i
for i, p in enumerate(XM):
    XOFF[p] = 40 + i
YP = [p for p in range(NPOP) if VEL[p][1] == 1]
Y0 = [p for p in range(NPOP) if VEL[p][1] == 0]
YM = [p for p in range(NPOP) if VEL[p][1] == -1]
SLOT = {}
for i, p in enumerate(Y0):
    SLOT[p] = i
for i, p in enumerate(YP):
    SLOT[p] = 24 + 2 * i
for i, p in enumerate(YM):
    SLOT[p] = 25 + 2 * i
NX, NY, NZ = 16, 128, 2
PAD = 8
RX = NX + 2 * PAD


def zflip(p):
    return abs(VEL[p][2])


def plane(p, z, r, count=8):
    first = (POS[p] * NZ + z) * RX + PAD + r
    return slice(first, first + count)


def collide(pops):
    f, g = pops[:19], [pops[19 + 7 * a : 26 + 7 * a] for a in range(3)]
    pairs = [(i, i + 1) for i in range(1, 19, 2)]
    even = [f[i] + f[j] for i, j in pairs]
    odd = [f[i] - f[j] for i, j in pairs]
    rho = f[0] + ((even[0] + even[1]) + (even[2] + even[3])) + ((even[4] + even[5]) + ((even[6] + even[7]) + even[8]))
    mom = []
    for a in range(3):
        terms = [(odd[k], VEL[pairs[k][0]][a]) for k in range(9) if VEL[pairs[k][0]][a]]
        total = terms[0][0]
        for value, sign in terms[1:]:
            total = total + value if sign > 0 else total - value
        mom.append(total)
    inv = 1.0 / rho
    u = [m * inv for m in mom]
    b = [((g[a][0] + g[a][1]) + (g[a][2] + g[a][3])) + ((g[a][4] + g[a][5]) + g[a][6]) for a in range(3)]
    half = 0.5 * (b[0] * b[0] + b[1] * b[1] + b[2] * b[2])
    diag = [mom[a] * u[a] - b[a] * b[a] + half for a in range(3)]
    cross = {(a, c): mom[a] * u[c] - b[a] * b[c] for a, c in ((0, 1), (0, 2), (1, 2))}
    trace = diag[0] + diag[1] + diag[2]
    base = (OM_F / 36.0) * (rho - 1.5 * trace)
    d45 = [(4.5 * OM_F / 36.0) * d for d in diag]
    c9 = {k: (9.0 * OM_F / 36.0) * v for k, v in cross.items()}
    m3 = [(3.0 * OM_F / 36.0) * m for m in mom]
    keep = 1.0 - OM_F
    out = [None] * NPOP
    out[0] = keep * f[0] + 12.0 * base
    for k, (i, j) in enumerate(pairs):
        c = VEL[i]
        axes = [a for a in range(3) if c[a]]
        if len(axes) == 1:
            s = 2.0 * (base + d45[axes[0]])
            t = 2.0 * m3[axes[0]]
        else:
            a, d = axes
            s = base + d45[a] + d45[d]
            if c[a] * c[d] > 0:
                s = s + c9[(a, d)]
            else:
                s = s - c9[(a, d)]
            first = m3[a] if c[a] > 0 else -m3[a]
            t = first + m3[d] if c[d] > 0 else first - m3[d]
        out[i] = keep * f[i] + (s + t)
        out[j] = keep * f[j] + (s - t)
    keep = 1.0 - OM_G
    for a in range(3):
        rest = (OM_G / 8.0) * b[a]
        out[19 + 7 * a] = keep * g[a][0] + 2.0 * rest
        for d in range(3):
            plus, minus = rest, rest
            if d != a:
                flux = (4.0 * OM_G / 8.0) * (u[d] * b[a] - b[d] * u[a])
                plus, minus = rest + flux, rest - flux
            out[19 + 7 * a + 1 + 2 * d] = keep * g[a][1 + 2 * d] + plus
            out[19 + 7 * a + 2 + 2 * d] = keep * g[a][2 + 2 * d] + minus
    return out


def exchange(sizes, f_hbm, g_hbm, q, xb, ao, yb, fv, gv, xs, load_sem, send_sem, recv_sem):
    nx_dev, ny_dev = sizes
    ix, iy = lax.axis_index("gx"), lax.axis_index("gy")

    def device(dx, dy):
        return (lax.rem(ix + dx + nx_dev, nx_dev), lax.rem(iy + dy + ny_dev, ny_dev))

    around = [(dx, dy) for dx in (-1, 0, 1) for dy in (-1, 0, 1) if dx or dy]
    barrier = pltpu.get_barrier_semaphore()
    for dx, dy in around:
        pl.semaphore_signal(barrier, inc=1, device_id=device(dx, dy), device_id_type=MESH)

    load_f = pltpu.make_async_copy(f_hbm, fv, load_sem.at[0])
    load_g = pltpu.make_async_copy(g_hbm, gv, load_sem.at[1])
    load_f.start()
    load_g.start()
    load_f.wait()
    load_g.wait()

    lane = lax.broadcasted_iota(jnp.int32, (8, NY), 1)
    for half in range(2):
        rows = slice(8 * half, 8 * half + 8)
        at = slice(PAD + 8 * half, PAD + 8 * half + 8)
        up = [jnp.zeros((8, NY), F32) for _ in range(NZ)]
        down = [jnp.zeros((8, NY), F32) for _ in range(NZ)]
        for z in range(NZ):
            pops = [fv[p, z, rows, :] for p in range(19)]
            pops += [gv[a, j, z, rows, :] for a in range(3) for j in range(7)]
            post = collide(pops)
            for p in range(NPOP):
                zz = z ^ zflip(p)
                q[plane(p, zz, 8 * half), :] = post[p]
                s = SLOT[p]
                if VEL[p][1] == 0:
                    moved = pltpu.roll(post[p], s + 1, 1)
                    up[zz] = jnp.where(lane == s, moved, up[zz])
                    down[zz] = jnp.where(lane == s + 1, moved, down[zz])
                elif VEL[p][1] == 1:
                    moved = pltpu.roll(post[p], s + 2, 1)
                    up[zz] = jnp.where((lane == s) | (lane == s + 1), moved, up[zz])
                else:
                    moved = pltpu.roll(post[p], s, 1)
                    down[zz] = jnp.where((lane == s) | (lane == s + 1), moved, down[zz])
        for z in range(NZ):
            ao[0, z, at, :] = up[z]
            ao[1, z, at, :] = down[z]

    def row(first, count, z, r):
        return q[pl.ds(first * NZ * RX + z * RX + PAD + r, count, stride=NZ * RX), :]

    for z in range(NZ):
        xs[0, z, 0:8, :] = row(0, 8, z, NX - 2)
        xs[0, z, 8:32, :] = row(8, 24, z, NX - 1)
        xs[0, z, 32:40, :] = row(0, 8, z, NX - 1)
        xs[1, z, 0:24, :] = row(8, 24, z, 0)
        xs[1, z, 24:32, :] = row(32, 8, z, 0)
        xs[1, z, 32:40, :] = row(32, 8, z, 1)
        xb[0, z, 40:48, :] = row(32, 8, z, 0)
        xb[1, z, 0:8, :] = row(0, 8, z, NX - 1)

    pl.semaphore_wait(barrier, len(around))
    low, high, own = slice(0, 8), slice(24, 32), slice(8, 24)
    first, last = slice(8, 16), slice(16, 24)
    moves = []
    for side, dy in ((0, 1), (1, -1)):
        moves.append((ao.at[side, :, last], yb.at[side, :, low], 1, dy))
        moves.append((ao.at[side, :, first], yb.at[side, :, high], -1, dy))
        moves.append((ao.at[side, :, own], yb.at[side, :, own], 0, dy))
    moves.append((xs.at[0], xb.at[0, :, 0:40], 1, 0))
    moves.append((xs.at[1], xb.at[1, :, 8:48], -1, 0))
    moves.append((ao.at[:, :, last], ao.at[:, :, low], 1, 0))
    moves.append((ao.at[:, :, first], ao.at[:, :, high], -1, 0))
    copies = [
        pltpu.make_async_remote_copy(
            src_ref=src, dst_ref=dst, send_sem=send_sem.at[k], recv_sem=recv_sem.at[k],
            device_id=device(dx, dy), device_id_type=MESH,
        )
        for k, (src, dst, dx, dy) in enumerate(moves)
    ]
    for copy in copies:
        copy.start()
    for copy in copies:
        copy.wait()
    for i in range(8):
        for z in range(NZ):
            q[plane(XP[i], z, -1, 1), :] = xb[0, z, 32 + i : 33 + i, :]
            q[plane(XM[i], z, NX, 1), :] = xb[1, z, 32 + i : 33 + i, :]


def finish(q, xb, ao, yb, f_hbm, g_hbm, w, tr, res, uu, fo, go, out_sem):
    lane = lax.broadcasted_iota(jnp.int32, (8, NY), 1)
    lanes = lax.broadcasted_iota(jnp.int32, (NZ * RX, NY), 1)
    mine = (lanes >= 25) & (lanes < 40) & (lanes % 2 == 1)
    left = jnp.where(mine, ao[1], yb[0])
    right = jnp.where(mine, ao[0], yb[1])
    right = pltpu.roll(right, NY - 1, 1)
    turned = jnp.concatenate([left, right], axis=0).T[0:40]
    tr[0] = turned
    tr[1] = pltpu.roll(turned, 1, 1)
    tr[2] = pltpu.roll(turned, NY - 1, 1)
    ring = collide([tr[VEL[p][0] % 3, SLOT[p] : SLOT[p] + 1, :] for p in range(NPOP)])
    for k in range(8):
        for base, p in ((0, YP[k]), (8, YM[k])):
            uu[base + k : base + k + 1, :] = pltpu.roll(ring[p], VEL[p][0] % NY, 1)
    sides = uu[...].T

    def edge(side, cx):
        a = yb[side, pl.ds(PAD - 1 - cx, 2, stride=RX), :]
        b = yb[side, pl.ds(PAD + NX - cx, 2, stride=RX), :]
        return jnp.concatenate([a, b], axis=0)

    edges = {(side, cx): edge(side, cx) for side in range(2) for cx in (-1, 0, 1)}
    lane4 = lax.broadcasted_iota(jnp.int32, (4, NY), 1)

    def shift_y(p, value, beside, at, lane):
        if VEL[p][1] == 1:
            return jnp.where(lane == 0, pltpu.roll(beside, (NY - at) % NY, 1), pltpu.roll(value, 1, 1))
        if VEL[p][1] == -1:
            return jnp.where(lane == NY - 1, pltpu.roll(beside, NY - 1 - at, 1), pltpu.roll(value, NY - 1, 1))
        return value

    def kth(p):
        return YP.index(p) if VEL[p][1] == 1 else YM.index(p)

    rows = []
    for p in range(NPOP):
        value = xb[pl.ds(XOFF[p], 4, stride=48), :]
        if VEL[p][1]:
            value = shift_y(p, value, edges[0 if VEL[p][1] == 1 else 1, VEL[p][0]], 25 + 2 * kth(p), lane4)
        rows.append(value)
    ring = collide(rows)
    for p in range(NPOP):
        for z in range(NZ):
            zz = z ^ zflip(p)
            if VEL[p][0] == 1:
                w[plane(p, zz, -1, 1), :] = ring[p][z : z + 1]
            elif VEL[p][0] == -1:
                w[plane(p, zz, NX, 1), :] = ring[p][2 + z : 3 + z]

    for z in range(NZ):
        for half in range(2):
            pops = []
            for p in range(NPOP):
                start = 8 * half - VEL[p][0]
                value = q[plane(p, z, start), :]
                if VEL[p][1]:
                    first = z * RX + PAD + start
                    beside = yb[0 if VEL[p][1] == 1 else 1, first : first + 8, :]
                    value = shift_y(p, value, beside, 25 + 2 * kth(p), lane)
                pops.append(value)
            post = collide(pops)
            for p in range(NPOP):
                w[plane(p, z ^ zflip(p), 8 * half), :] = post[p]

    res[...] = sides
    for p in range(NPOP):
        for z in range(NZ):
            for half in range(2):
                value = w[plane(p, z, 8 * half - VEL[p][0]), :]
                if VEL[p][1]:
                    side, at = (0, kth(p)) if VEL[p][1] == 1 else (1, 8 + kth(p))
                    first = (side * NZ + (z ^ zflip(p))) * RX + PAD + 8 * half
                    value = shift_y(p, value, res[first : first + 8, :], at, lane)
                to = slice(8 * half, 8 * half + 8)
                if p < 19:
                    fo[p, z, to, :] = value
                else:
                    go[(p - 19) // 7, (p - 19) % 7, z, to, :] = value
    store_f = pltpu.make_async_copy(fo, f_hbm, out_sem.at[0])
    store_g = pltpu.make_async_copy(go, g_hbm, out_sem.at[1])
    store_f.start()
    store_g.start()
    store_f.wait()
    store_g.wait()


def per_device(sizes, fluid_pops, magnet_pops):
    vmem = pl.BlockSpec(memory_space=pltpu.VMEM)
    hbm = pl.BlockSpec(memory_space=pltpu.HBM)
    fluid, magnet = (19, NZ, NX, NY), (3, 7, NZ, NX, NY)
    halos = [
        pltpu.VMEM((NPOP * NZ * RX, NY), F32),
        pltpu.VMEM((2, NZ, 48, NY), F32),
        pltpu.VMEM((2, NZ, RX, NY), F32),
        pltpu.VMEM((2, NZ, RX, NY), F32),
    ]
    q, xb, ao, yb = pl.pallas_call(
        functools.partial(exchange, sizes),
        out_shape=halos,
        in_specs=[hbm] * 2,
        out_specs=[vmem] * 4,
        scratch_shapes=[
            pltpu.VMEM(fluid, F32),
            pltpu.VMEM(magnet, F32),
            pltpu.VMEM((2, NZ, 40, NY), F32),
            pltpu.SemaphoreType.DMA((2,)),
            pltpu.SemaphoreType.DMA((10,)),
            pltpu.SemaphoreType.DMA((10,)),
        ],
        compiler_params=pltpu.CompilerParams(
            collective_id=0, has_side_effects=True, vmem_limit_bytes=VMEM_LIMIT
        ),
    )(fluid_pops, magnet_pops)
    return pl.pallas_call(
        finish,
        out_shape=[jax.ShapeDtypeStruct(fluid, F32), jax.ShapeDtypeStruct(magnet, F32)],
        in_specs=[vmem] * 4,
        out_specs=[hbm] * 2,
        scratch_shapes=[
            pltpu.VMEM((NPOP * NZ * RX, NY), F32),
            pltpu.VMEM((3, 40, NY), F32),
            pltpu.VMEM((NY, NY), F32),
            pltpu.VMEM((NY, NY), F32),
            pltpu.VMEM(fluid, F32),
            pltpu.VMEM(magnet, F32),
            pltpu.SemaphoreType.DMA((2,)),
        ],
        compiler_params=pltpu.CompilerParams(vmem_limit_bytes=VMEM_LIMIT),
    )(
        q,
        xb.reshape(2 * NZ * 48, NY),
        ao.reshape(2, NZ * RX, NY),
        yb.reshape(2, NZ * RX, NY),
    )


VMEM_LIMIT = 48 << 20


def solution(mesh):
    specs = (P(None, None, "gx", "gy"), P(None, None, None, "gx", "gy"))
    return jax.shard_map(
        functools.partial(per_device, (mesh.shape["gx"], mesh.shape["gy"])),
        mesh=mesh,
        in_specs=specs,
        out_specs=specs,
        check_vma=False,
    )
```

time: 88.9 us -> 23.3 us (0.26)
  the two profiles are of different devices: /device:TPU:24 before, /device:TPU:1 now
where the time goes in v1:
time: 23.3 us; the launch traced here: 23.1 us
  Pallas kernels  20.5 us (88%)
  local copies, waits for them, and re-layouts  1.94 us (8%)
  between operations  0.65 us (3%)
    pallas_call x1, Pallas kernels, per_device(): pl.pallas_call(functools.partial(exchange, sizes), out_shape=halos, in_sp...  18.9 us
    unnamed x4, local copies, waits for them, and re-layouts  1.94 us
    pallas_call x1, Pallas kernels, per_device(): pl.pallas_call(finish, out_shape=[jax.ShapeDtypeStruct(fluid, F32), jax.S...  1.65 us

profile of v1, /device:TPU:1, one launch (start us, length us, event | category | flops | bytes accessed | tf_op | source)
XLA Modules:
  0.0 23.1 jit_solution(12290435504858145334)
XLA Ops:
  0.6 0.0 copy-start
  0.6 1.0 %copy-done = f32[3,7,2,16,128]{4,3,2,1,0:T(8,128)S(1)} copy-done((f32[3,7,2,16,128]{4,3,2,1,0:T(8,128)S(1)}, f32[3,7,2,16,128]{4,3,2,1,0:T(8,128)}, u32[]{:S(2)}) %copy-start) | copy-done | bytes 344088
  1.6 0.0 copy-start.1
  1.6 1.0 %copy-done.1 = f32[19,2,16,128]{3,2,1,0:T(8,128)S(1)} copy-done((f32[19,2,16,128]{3,2,1,0:T(8,128)S(1)}, f32[19,2,16,128]{3,2,1,0:T(8,128)}, u32[]{:S(2)}) %copy-start.1) | copy-done | bytes 311320
  2.6 18.9 %shard_map.41 = (f32[2560,128]{1,0:T(8,128)S(1)}, f32[2,2,48,128]{3,2,1,0:T(8,128)S(1)}, f32[2,2,32,128]{3,2,1,0:T(8,128)S(1)}, f32[2,2,32,128]{3,2,1,0:T(8,128)S(1)}) custom-call(f32[19,2,16,128]{3,2,1,0:T(8,128)S(1)} %copy-done.1, f32[3,7,2,16,128]{4,3,2,1,0:T(8,128)S(1)} %copy-done), custom_call_target="tpu_custom_call" | custom-call | tf_op jit(solution)/shard_map/pallas_call | solution.py:305
  21.5 1.6 %shard_map.42 = (f32[19,2,16,128]{3,2,1,0:T(8,128)}, f32[3,7,2,16,128]{4,3,2,1,0:T(8,128)}) custom-call(f32[2560,128]{1,0:T(8,128)S(1)} %get-tuple-element.6.q, f32[192,128]{1,0:T(8,128)S(1)} %bitcast.3, f32[2,64,128]{2,1,0:T(8,128)S(1)} %bitcast.4, f32[2,64,128]{2,1,0:T(8,128)S(1)} %bitcast.5), custom_call_target="tpu_custom_call" | custom-call | tf_op jit(solution)/shard_map/pallas_call | solution.py:322
Async XLA Ops:
  0.6 1.0 %copy-start = (f32[3,7,2,16,128]{4,3,2,1,0:T(8,128)S(1)}, f32[3,7,2,16,128]{4,3,2,1,0:T(8,128)}, u32[]{:S(2)}) copy-start(f32[3,7,2,16,128]{4,3,2,1,0:T(8,128)} %g_hbm.1) | copy-start | bytes 1032196
  1.6 1.0 %copy-start.1 = (f32[19,2,16,128]{3,2,1,0:T(8,128)S(1)}, f32[19,2,16,128]{3,2,1,0:T(8,128)}, u32[]{:S(2)}) copy-start(f32[19,2,16,128]{3,2,1,0:T(8,128)} %f_hbm.1) | copy-start | bytes 933892

commit v2 on v1

--- a/solution.py
+++ b/solution.py
@@ -116,22 +116,46 @@
     return out
 
 
-def exchange(sizes, f_hbm, g_hbm, q, xb, ao, yb, fv, gv, xs, load_sem, send_sem, recv_sem):
+def exchange(sizes, f_hbm, g_hbm, q, xb, ao, yb, fv, gv, xs, load_sem, send_sem, recv_sem, ready):
     nx_dev, ny_dev = sizes
     ix, iy = lax.axis_index("gx"), lax.axis_index("gy")
 
     def device(dx, dy):
         return (lax.rem(ix + dx + nx_dev, nx_dev), lax.rem(iy + dy + ny_dev, ny_dev))
 
-    around = [(dx, dy) for dx in (-1, 0, 1) for dy in (-1, 0, 1) if dx or dy]
-    barrier = pltpu.get_barrier_semaphore()
-    for dx, dy in around:
-        pl.semaphore_signal(barrier, inc=1, device_id=device(dx, dy), device_id_type=MESH)
+    block = SEAM if ny_dev % SEAM == 0 else ny_dev
+    place = lax.rem(iy, block)
+    is_first, is_last, is_before = place == 0, place == block - 1, place == block - 2
 
     load_f = pltpu.make_async_copy(f_hbm, fv, load_sem.at[0])
     load_g = pltpu.make_async_copy(g_hbm, gv, load_sem.at[1])
     load_f.start()
     load_g.start()
+
+    barrier = pltpu.get_barrier_semaphore()
+
+    def greet(steps, semaphore):
+        for dx, dy in steps:
+            pl.semaphore_signal(semaphore, inc=1, device_id=device(dx, dy), device_id_type=MESH)
+
+    beside = [(-1, 0), (1, 0)]
+    above = [(-1, 1), (0, 1), (1, 1)]
+    below = [(-1, -1), (0, -1), (1, -1)]
+
+    @pl.when(is_last)
+    def _():
+        greet(below, barrier)
+        pl.semaphore_wait(barrier, 3)
+        greet(above, ready)
+
+    @pl.when(jnp.logical_not(is_last))
+    def _():
+        greet(below + beside, barrier)
+
+        @pl.when(jnp.logical_not(is_before))
+        def _():
+            greet(above, barrier)
+
     load_f.wait()
     load_g.wait()
 
@@ -163,6 +187,51 @@
             ao[0, z, at, :] = up[z]
             ao[1, z, at, :] = down[z]
 
+    low, high, own = slice(0, 8), slice(24, 32), slice(8, 24)
+    first, last = slice(8, 16), slice(16, 24)
+    slots = iter(range(10))
+
+    def to(src, dst, dx, dy):
+        k = next(slots)
+        return pltpu.make_async_remote_copy(
+            src_ref=src, dst_ref=dst, send_sem=send_sem.at[k], recv_sem=recv_sem.at[k],
+            device_id=device(dx, dy), device_id_type=MESH,
+        )
+
+    def to_row(side, dy):
+        return [
+            to(ao.at[side, :, last], yb.at[side, :, low], 1, dy),
+            to(ao.at[side, :, first], yb.at[side, :, high], -1, dy),
+            to(ao.at[side, :, own], yb.at[side, :, own], 0, dy),
+        ]
+
+    to_above = to_row(0, 1)
+    to_below = to_row(1, -1)
+    to_beside = [
+        to(xs.at[0], xb.at[0, :, 0:40], 1, 0),
+        to(xs.at[1], xb.at[1, :, 8:48], -1, 0),
+        to(ao.at[:, :, last], ao.at[:, :, low], 1, 0),
+        to(ao.at[:, :, first], ao.at[:, :, high], -1, 0),
+    ]
+
+    def start(copies):
+        for copy in copies:
+            copy.start()
+
+    @pl.when(is_first)
+    def _():
+        pl.semaphore_wait(barrier, 5)
+
+    @pl.when(jnp.logical_not(is_first | is_last))
+    def _():
+        pl.semaphore_wait(barrier, 8)
+
+    @pl.when(is_before)
+    def _():
+        greet([(0, 1)], ready)
+
+    start(to_above)
+
     def row(first, count, z, r):
         return q[pl.ds(first * NZ * RX + z * RX + PAD + r, count, stride=NZ * RX), :]
 
@@ -176,28 +245,21 @@
         xb[0, z, 40:48, :] = row(32, 8, z, 0)
         xb[1, z, 0:8, :] = row(0, 8, z, NX - 1)
 
-    pl.semaphore_wait(barrier, len(around))
-    low, high, own = slice(0, 8), slice(24, 32), slice(8, 24)
-    first, last = slice(8, 16), slice(16, 24)
-    moves = []
-    for side, dy in ((0, 1), (1, -1)):
-        moves.append((ao.at[side, :, last], yb.at[side, :, low], 1, dy))
-        moves.append((ao.at[side, :, first], yb.at[side, :, high], -1, dy))
-        moves.append((ao.at[side, :, own], yb.at[side, :, own], 0, dy))
-    moves.append((xs.at[0], xb.at[0, :, 0:40], 1, 0))
-    moves.append((xs.at[1], xb.at[1, :, 8:48], -1, 0))
-    moves.append((ao.at[:, :, last], ao.at[:, :, low], 1, 0))
-    moves.append((ao.at[:, :, first], ao.at[:, :, high], -1, 0))
-    copies = [
-        pltpu.make_async_remote_copy(
-            src_ref=src, dst_ref=dst, send_sem=send_sem.at[k], recv_sem=recv_sem.at[k],
-            device_id=device(dx, dy), device_id_type=MESH,
-        )
-        for k, (src, dst, dx, dy) in enumerate(moves)
-    ]
-    for copy in copies:
-        copy.start()
-    for copy in copies:
+    @pl.when(jnp.logical_not(is_last))
+    def _():
+        start(to_beside)
+
+    @pl.when(is_first)
+    def _():
+        pl.semaphore_wait(ready, 3)
+
+    @pl.when(is_last)
+    def _():
+        pl.semaphore_wait(ready, 1)
+        start(to_beside)
+
+    start(to_below)
+    for copy in to_above + to_below + to_beside:
         copy.wait()
     for i in range(8):
         for z in range(NZ):
@@ -314,11 +376,15 @@
             pltpu.SemaphoreType.DMA((2,)),
             pltpu.SemaphoreType.DMA((10,)),
             pltpu.SemaphoreType.DMA((10,)),
+            pltpu.SemaphoreType.REGULAR,
         ],
         compiler_params=pltpu.CompilerParams(
             collective_id=0, has_side_effects=True, vmem_limit_bytes=VMEM_LIMIT
         ),
-    )(fluid_pops, magnet_pops)
+    )(
+        pltpu.with_memory_space_constraint(fluid_pops, pltpu.HBM),
+        pltpu.with_memory_space_constraint(magnet_pops, pltpu.HBM),
+    )
     return pl.pallas_call(
         finish,
         out_shape=[jax.ShapeDtypeStruct(fluid, F32), jax.ShapeDtypeStruct(magnet, F32)],
@@ -343,6 +409,7 @@
 
 
 VMEM_LIMIT = 48 << 20
+SEAM = 16
 
 
 def solution(mesh):

time: 23.3 us -> 19.3 us (0.83)
  the two profiles are of different devices: /device:TPU:1 before, /device:TPU:24 now
where the time goes in v2:
time: 19.3 us; the launch traced here: 19.1 us
  Pallas kernels  18.5 us (96%)
  between operations  0.64 us (3%)
    pallas_call x1, Pallas kernels, per_device(): pl.pallas_call(functools.partial(exchange, sizes), out_shape=halos, in_sp...  16.8 us
    pallas_call x1, Pallas kernels, per_device(): pl.pallas_call(finish, out_shape=[jax.ShapeDtypeStruct(fluid, F32), jax.S...  1.65 us

profile of v2, /device:TPU:24, one launch (start us, length us, event | category | flops | bytes accessed | tf_op | source)
XLA Modules:
  0.0 19.1 jit_solution(11081561204009365890)
XLA Ops:
  0.6 16.8 %shard_map.41 = (f32[2560,128]{1,0:T(8,128)S(1)}, f32[2,2,48,128]{3,2,1,0:T(8,128)S(1)}, f32[2,2,32,128]{3,2,1,0:T(8,128)S(1)}, f32[2,2,32,128]{3,2,1,0:T(8,128)S(1)}) custom-call(f32[19,2,16,128]{3,2,1,0:T(8,128)} %f_hbm.1, f32[3,7,2,16,128]{4,3,2,1,0:T(8,128)} %g_hbm.1), custom_call_target="tpu_custom_call" | custom-call | tf_op jit(solution)/shard_map/pallas_call | solution.py:367
  17.5 1.6 %shard_map.42 = (f32[19,2,16,128]{3,2,1,0:T(8,128)}, f32[3,7,2,16,128]{4,3,2,1,0:T(8,128)}) custom-call(f32[2560,128]{1,0:T(8,128)S(1)} %get-tuple-element.6.q, f32[192,128]{1,0:T(8,128)S(1)} %bitcast.3, f32[2,64,128]{2,1,0:T(8,128)S(1)} %bitcast.4, f32[2,64,128]{2,1,0:T(8,128)S(1)} %bitcast.5), custom_call_target="tpu_custom_call" | custom-call | tf_op jit(solution)/shard_map/pallas_call | solution.py:388

commit v3 on v2

--- a/solution.py
+++ b/solution.py
@@ -116,7 +116,7 @@
     return out
 
 
-def exchange(sizes, f_hbm, g_hbm, q, xb, ao, yb, fv, gv, xs, load_sem, send_sem, recv_sem, ready):
+def exchange(sizes, f_hbm, g_hbm, fo, go, ao, yb, fv, gv, q, w, xs, xb, load_sem, send_sem, recv_sem, ready):
     nx_dev, ny_dev = sizes
     ix, iy = lax.axis_index("gx"), lax.axis_index("gy")
 
@@ -127,10 +127,17 @@
     place = lax.rem(iy, block)
     is_first, is_last, is_before = place == 0, place == block - 1, place == block - 2
 
-    load_f = pltpu.make_async_copy(f_hbm, fv, load_sem.at[0])
-    load_g = pltpu.make_async_copy(g_hbm, gv, load_sem.at[1])
-    load_f.start()
-    load_g.start()
+    loads = []
+    for half in range(2):
+        for z in range(NZ):
+            rows = slice(8 * half, 8 * half + 8)
+            piece = (
+                pltpu.make_async_copy(f_hbm.at[:, z, rows], fv.at[:, z, rows], load_sem.at[half, z, 0]),
+                pltpu.make_async_copy(g_hbm.at[:, :, z, rows], gv.at[:, :, z, rows], load_sem.at[half, z, 1]),
+            )
+            loads.append(piece)
+            for copy in piece:
+                copy.start()
 
     barrier = pltpu.get_barrier_semaphore()
 
@@ -156,8 +163,36 @@
         def _():
             greet(above, barrier)
 
-    load_f.wait()
-    load_g.wait()
+    low, high, own = slice(0, 8), slice(24, 32), slice(8, 24)
+    first, last = slice(8, 16), slice(16, 24)
+    slots = iter(range(10))
+
+    def to(src, dst, dx, dy):
+        k = next(slots)
+        return pltpu.make_async_remote_copy(
+            src_ref=src, dst_ref=dst, send_sem=send_sem.at[k], recv_sem=recv_sem.at[k],
+            device_id=device(dx, dy), device_id_type=MESH,
+        )
+
+    def to_row(side, dy):
+        return [
+            to(ao.at[:, first], yb.at[side, :, high], -1, dy),
+            to(ao.at[:, last], yb.at[side, :, low], 1, dy),
+            to(ao.at[:, own], yb.at[side, :, own], 0, dy),
+        ]
+
+    to_above = to_row(0, 1)
+    to_below = to_row(1, -1)
+    to_beside = [
+        to(xs.at[0], xb.at[0, :, 0:40], 1, 0),
+        to(xs.at[1], xb.at[1, :, 8:48], -1, 0),
+        to(ao.at[:, last], ao.at[:, low], 1, 0),
+        to(ao.at[:, first], ao.at[:, high], -1, 0),
+    ]
+
+    def start(copies):
+        for copy in copies:
+            copy.start()
 
     lane = lax.broadcasted_iota(jnp.int32, (8, NY), 1)
     for half in range(2):
@@ -166,6 +201,8 @@
         up = [jnp.zeros((8, NY), F32) for _ in range(NZ)]
         down = [jnp.zeros((8, NY), F32) for _ in range(NZ)]
         for z in range(NZ):
+            for copy in loads[half * NZ + z]:
+                copy.wait()
             pops = [fv[p, z, rows, :] for p in range(19)]
             pops += [gv[a, j, z, rows, :] for a in range(3) for j in range(7)]
             post = collide(pops)
@@ -184,39 +221,14 @@
                     moved = pltpu.roll(post[p], s, 1)
                     down[zz] = jnp.where((lane == s) | (lane == s + 1), moved, down[zz])
         for z in range(NZ):
-            ao[0, z, at, :] = up[z]
-            ao[1, z, at, :] = down[z]
-
-    low, high, own = slice(0, 8), slice(24, 32), slice(8, 24)
-    first, last = slice(8, 16), slice(16, 24)
-    slots = iter(range(10))
-
-    def to(src, dst, dx, dy):
-        k = next(slots)
-        return pltpu.make_async_remote_copy(
-            src_ref=src, dst_ref=dst, send_sem=send_sem.at[k], recv_sem=recv_sem.at[k],
-            device_id=device(dx, dy), device_id_type=MESH,
-        )
-
-    def to_row(side, dy):
-        return [
-            to(ao.at[side, :, last], yb.at[side, :, low], 1, dy),
-            to(ao.at[side, :, first], yb.at[side, :, high], -1, dy),
-            to(ao.at[side, :, own], yb.at[side, :, own], 0, dy),
-        ]
-
-    to_above = to_row(0, 1)
-    to_below = to_row(1, -1)
-    to_beside = [
-        to(xs.at[0], xb.at[0, :, 0:40], 1, 0),
-        to(xs.at[1], xb.at[1, :, 8:48], -1, 0),
-        to(ao.at[:, :, last], ao.at[:, :, low], 1, 0),
-        to(ao.at[:, :, first], ao.at[:, :, high], -1, 0),
-    ]
-
-    def start(copies):
-        for copy in copies:
-            copy.start()
+            here = jnp.where((lane < 24) | ((lane < 40) & (lane % 2 == 0)), up[z], down[z])
+            there = jnp.where((lane >= 25) & (lane < 40) & (lane % 2 == 1), up[z], down[z])
+            ao[z, at, :] = jnp.where(lane < 64, here, pltpu.roll(there, 63, 1))
+        if half == 0:
+
+            @pl.when(is_last)
+            def _():
+                start(to_above[:1])
 
     @pl.when(is_first)
     def _():
@@ -230,7 +242,11 @@
     def _():
         greet([(0, 1)], ready)
 
-    start(to_above)
+    @pl.when(jnp.logical_not(is_last))
+    def _():
+        start(to_above[:1])
+
+    start(to_above[1:])
 
     def row(first, count, z, r):
         return q[pl.ds(first * NZ * RX + z * RX + PAD + r, count, stride=NZ * RX), :]
@@ -245,135 +261,135 @@
         xb[0, z, 40:48, :] = row(32, 8, z, 0)
         xb[1, z, 0:8, :] = row(0, 8, z, NX - 1)
 
-    @pl.when(jnp.logical_not(is_last))
-    def _():
-        start(to_beside)
-
-    @pl.when(is_first)
-    def _():
-        pl.semaphore_wait(ready, 3)
-
     @pl.when(is_last)
     def _():
         pl.semaphore_wait(ready, 1)
-        start(to_beside)
-
-    start(to_below)
-    for copy in to_above + to_below + to_beside:
+
+    start(to_beside)
+
+    @pl.when(jnp.logical_not(is_first))
+    def _():
+        start(to_below)
+
+    for copy in to_beside:
         copy.wait()
+
+    def turn(p, value):
+        return pltpu.roll(value, VEL[p][1] % NY, 1) if VEL[p][1] else value
+
     for i in range(8):
         for z in range(NZ):
             q[plane(XP[i], z, -1, 1), :] = xb[0, z, 32 + i : 33 + i, :]
             q[plane(XM[i], z, NX, 1), :] = xb[1, z, 32 + i : 33 + i, :]
-
-
-def finish(q, xb, ao, yb, f_hbm, g_hbm, w, tr, res, uu, fo, go, out_sem):
-    lane = lax.broadcasted_iota(jnp.int32, (8, NY), 1)
-    lanes = lax.broadcasted_iota(jnp.int32, (NZ * RX, NY), 1)
-    mine = (lanes >= 25) & (lanes < 40) & (lanes % 2 == 1)
-    left = jnp.where(mine, ao[1], yb[0])
-    right = jnp.where(mine, ao[0], yb[1])
-    right = pltpu.roll(right, NY - 1, 1)
-    turned = jnp.concatenate([left, right], axis=0).T[0:40]
-    tr[0] = turned
-    tr[1] = pltpu.roll(turned, 1, 1)
-    tr[2] = pltpu.roll(turned, NY - 1, 1)
-    ring = collide([tr[VEL[p][0] % 3, SLOT[p] : SLOT[p] + 1, :] for p in range(NPOP)])
-    for k in range(8):
-        for base, p in ((0, YP[k]), (8, YM[k])):
-            uu[base + k : base + k + 1, :] = pltpu.roll(ring[p], VEL[p][0] % NY, 1)
-    sides = uu[...].T
-
-    def edge(side, cx):
-        a = yb[side, pl.ds(PAD - 1 - cx, 2, stride=RX), :]
-        b = yb[side, pl.ds(PAD + NX - cx, 2, stride=RX), :]
-        return jnp.concatenate([a, b], axis=0)
-
-    edges = {(side, cx): edge(side, cx) for side in range(2) for cx in (-1, 0, 1)}
-    lane4 = lax.broadcasted_iota(jnp.int32, (4, NY), 1)
-
-    def shift_y(p, value, beside, at, lane):
-        if VEL[p][1] == 1:
-            return jnp.where(lane == 0, pltpu.roll(beside, (NY - at) % NY, 1), pltpu.roll(value, 1, 1))
-        if VEL[p][1] == -1:
-            return jnp.where(lane == NY - 1, pltpu.roll(beside, NY - 1 - at, 1), pltpu.roll(value, NY - 1, 1))
-        return value
-
-    def kth(p):
-        return YP.index(p) if VEL[p][1] == 1 else YM.index(p)
-
-    rows = []
+    edges = []
     for p in range(NPOP):
-        value = xb[pl.ds(XOFF[p], 4, stride=48), :]
-        if VEL[p][1]:
-            value = shift_y(p, value, edges[0 if VEL[p][1] == 1 else 1, VEL[p][0]], 25 + 2 * kth(p), lane4)
-        rows.append(value)
-    ring = collide(rows)
+        at = slice(XOFF[p], XOFF[p] + 1)
+        edges.append(turn(p, jnp.concatenate([xb[side, z, at, :] for side in range(2) for z in range(NZ)], axis=0)))
+    edges = collide(edges)
     for p in range(NPOP):
         for z in range(NZ):
             zz = z ^ zflip(p)
             if VEL[p][0] == 1:
-                w[plane(p, zz, -1, 1), :] = ring[p][z : z + 1]
+                w[plane(p, zz, -1, 1), :] = edges[p][z : z + 1]
             elif VEL[p][0] == -1:
-                w[plane(p, zz, NX, 1), :] = ring[p][2 + z : 3 + z]
-
+                w[plane(p, zz, NX, 1), :] = edges[p][NZ + z : NZ + z + 1]
     for z in range(NZ):
         for half in range(2):
-            pops = []
-            for p in range(NPOP):
-                start = 8 * half - VEL[p][0]
-                value = q[plane(p, z, start), :]
-                if VEL[p][1]:
-                    first = z * RX + PAD + start
-                    beside = yb[0 if VEL[p][1] == 1 else 1, first : first + 8, :]
-                    value = shift_y(p, value, beside, 25 + 2 * kth(p), lane)
-                pops.append(value)
-            post = collide(pops)
+            post = collide([turn(p, q[plane(p, z, 8 * half - VEL[p][0]), :]) for p in range(NPOP)])
             for p in range(NPOP):
                 w[plane(p, z ^ zflip(p), 8 * half), :] = post[p]
-
-    res[...] = sides
     for p in range(NPOP):
         for z in range(NZ):
             for half in range(2):
-                value = w[plane(p, z, 8 * half - VEL[p][0]), :]
-                if VEL[p][1]:
-                    side, at = (0, kth(p)) if VEL[p][1] == 1 else (1, 8 + kth(p))
-                    first = (side * NZ + (z ^ zflip(p))) * RX + PAD + 8 * half
-                    value = shift_y(p, value, res[first : first + 8, :], at, lane)
-                to = slice(8 * half, 8 * half + 8)
+                value = turn(p, w[plane(p, z, 8 * half - VEL[p][0]), :])
+                rows = slice(8 * half, 8 * half + 8)
                 if p < 19:
-                    fo[p, z, to, :] = value
+                    fo[p, z, rows, :] = value
                 else:
-                    go[(p - 19) // 7, (p - 19) % 7, z, to, :] = value
-    store_f = pltpu.make_async_copy(fo, f_hbm, out_sem.at[0])
-    store_g = pltpu.make_async_copy(go, g_hbm, out_sem.at[1])
-    store_f.start()
-    store_g.start()
-    store_f.wait()
-    store_g.wait()
+                    go[(p - 19) // 7, (p - 19) % 7, z, rows, :] = value
+
+    @pl.when(is_first)
+    def _():
+        pl.semaphore_wait(ready, 3)
+        start(to_below)
+
+    for copy in to_above + to_below:
+        copy.wait()
+
+
+def finish(fi, gi, ao, yb, f_hbm, g_hbm, tr, uu, mg, fo, go, out_sem):
+    lane = lax.broadcasted_iota(jnp.int32, (NZ * RX, NY), 1)
+    near_right = (lane < 24) | (((lane < 40) | ((lane >= 88) & (lane < 104))) & (lane % 2 == 0))
+    tr[0:NY, 0 : NZ * RX] = jnp.where(near_right, yb[0], ao[...]).T
+    tr[NY:, 0 : NZ * RX] = jnp.where(near_right, ao[...], yb[1]).T
+
+    def turn(p, value):
+        return pltpu.roll(value, VEL[p][0] % NY, 1) if VEL[p][0] else value
+
+    post = collide([turn(p, tr[pl.ds(SLOT[p], 4, stride=64), :]) for p in range(NPOP)])
+    shift = {}
+    for p in range(NPOP):
+        if VEL[p][1] == 0:
+            s = 2 * SLOT[p]
+            uu[s : s + 1, :] = post[p][2:3]
+            uu[s + 1 : s + 2, :] = post[p][1:2]
+            shift[p] = NY - 1 - s
+        elif VEL[p][1] == 1:
+            s = 48 + (SLOT[p] - 24)
+            uu[s : s + 2, :] = post[p][0:2]
+            shift[p] = NY - s
+        else:
+            s = 64 + (SLOT[p] - 25)
+            uu[s : s + 2, :] = post[p][2:4]
+            shift[p] = NY - 2 - s
+    mg[...] = uu[:, 0 : NZ * RX].T
+    lane = lax.broadcasted_iota(jnp.int32, (8, NY), 1)
+    masks = {0: (lane == 0) | (lane == NY - 1), 1: lane < 2, -1: lane >= NY - 2}
+    stores = [
+        (9, fo.at[0:10], f_hbm.at[0:10]),
+        (18, fo.at[10:19], f_hbm.at[10:19]),
+        (25, go.at[0], g_hbm.at[0]),
+        (32, go.at[1], g_hbm.at[1]),
+        (39, go.at[2], g_hbm.at[2]),
+    ]
+    copies = []
+    for p in range(NPOP):
+        for z in range(NZ):
+            for half in range(2):
+                start = (z ^ zflip(p)) * RX + PAD + 8 * half - VEL[p][0]
+                patch = pltpu.roll(mg[start : start + 8, :], shift[p], 1)
+                rows = slice(8 * half, 8 * half + 8)
+                if p < 19:
+                    fo[p, z, rows, :] = jnp.where(masks[VEL[p][1]], patch, fi[p, z, rows, :])
+                else:
+                    a, j = (p - 19) // 7, (p - 19) % 7
+                    go[a, j, z, rows, :] = jnp.where(masks[VEL[p][1]], patch, gi[a, j, z, rows, :])
+        for k, (after, src, dst) in enumerate(stores):
+            if after == p:
+                copies.append(pltpu.make_async_copy(src, dst, out_sem.at[k]))
+                copies[-1].start()
+    for copy in copies:
+        copy.wait()
 
 
 def per_device(sizes, fluid_pops, magnet_pops):
     vmem = pl.BlockSpec(memory_space=pltpu.VMEM)
     hbm = pl.BlockSpec(memory_space=pltpu.HBM)
     fluid, magnet = (19, NZ, NX, NY), (3, 7, NZ, NX, NY)
-    halos = [
-        pltpu.VMEM((NPOP * NZ * RX, NY), F32),
-        pltpu.VMEM((2, NZ, 48, NY), F32),
-        pltpu.VMEM((2, NZ, RX, NY), F32),
-        pltpu.VMEM((2, NZ, RX, NY), F32),
-    ]
-    q, xb, ao, yb = pl.pallas_call(
+    columns = (NZ, RX, NY)
+    fo, go, ao, yb = pl.pallas_call(
         functools.partial(exchange, sizes),
-        out_shape=halos,
+        out_shape=[pltpu.VMEM(shape, F32) for shape in (fluid, magnet, columns, (2, *columns))],
         in_specs=[hbm] * 2,
         out_specs=[vmem] * 4,
         scratch_shapes=[
             pltpu.VMEM(fluid, F32),
             pltpu.VMEM(magnet, F32),
+            pltpu.VMEM((NPOP * NZ * RX, NY), F32),
+            pltpu.VMEM((NPOP * NZ * RX, NY), F32),
             pltpu.VMEM((2, NZ, 40, NY), F32),
-            pltpu.SemaphoreType.DMA((2,)),
+            pltpu.VMEM((2, NZ, 48, NY), F32),
+            pltpu.SemaphoreType.DMA((2, NZ, 2)),
             pltpu.SemaphoreType.DMA((10,)),
             pltpu.SemaphoreType.DMA((10,)),
             pltpu.SemaphoreType.REGULAR,
@@ -391,21 +407,15 @@
         in_specs=[vmem] * 4,
         out_specs=[hbm] * 2,
         scratch_shapes=[
-            pltpu.VMEM((NPOP * NZ * RX, NY), F32),
-            pltpu.VMEM((3, 40, NY), F32),
+            pltpu.VMEM((2 * NY, NY), F32),
             pltpu.VMEM((NY, NY), F32),
-            pltpu.VMEM((NY, NY), F32),
+            pltpu.VMEM((NZ * RX, NY), F32),
             pltpu.VMEM(fluid, F32),
             pltpu.VMEM(magnet, F32),
-            pltpu.SemaphoreType.DMA((2,)),
+            pltpu.SemaphoreType.DMA((5,)),
         ],
         compiler_params=pltpu.CompilerParams(vmem_limit_bytes=VMEM_LIMIT),
-    )(
-        q,
-        xb.reshape(2 * NZ * 48, NY),
-        ao.reshape(2, NZ * RX, NY),
-        yb.reshape(2, NZ * RX, NY),
-    )
+    )(fo, go, ao.reshape(NZ * RX, NY), yb.reshape(2, NZ * RX, NY))
 
 
 VMEM_LIMIT = 48 << 20

time: 19.3 us -> 19 us (0.984)
  Pallas kernels: 18.5 us -> 18.2 us
    pallas_call x1, Pallas kernels: 1.65 us -> 1.42 us  [per_device(): pl.pallas_call(finish, out_shape=[jax.ShapeDtypeStruct(fluid, F32), jax.S...]
where the time goes in v3:
time: 19 us; the launch traced here: 18.8 us
  Pallas kernels  18.2 us (96%)
  between operations  0.64 us (3%)
    pallas_call x1, Pallas kernels, per_device(): pl.pallas_call(functools.partial(exchange, sizes), out_shape=[pltpu.VMEM(...  16.8 us
    pallas_call x1, Pallas kernels, per_device(): pl.pallas_call(finish, out_shape=[jax.ShapeDtypeStruct(fluid, F32), jax.S...  1.42 us

profile of v3, /device:TPU:24, one launch (start us, length us, event | category | flops | bytes accessed | tf_op | source)
XLA Modules:
  0.0 18.8 jit_solution(5802577213774097613)
XLA Ops:
  0.6 16.8 %shard_map.41 = (f32[19,2,16,128]{3,2,1,0:T(8,128)S(1)}, f32[3,7,2,16,128]{4,3,2,1,0:T(8,128)S(1)}, f32[2,32,128]{2,1,0:T(8,128)S(1)}, f32[2,2,32,128]{3,2,1,0:T(8,128)S(1)}) custom-call(f32[19,2,16,128]{3,2,1,0:T(8,128)} %f_hbm.1, f32[3,7,2,16,128]{4,3,2,1,0:T(8,128)} %g_hbm.1), custom_call_target="tpu_custom_call" | custom-call | tf_op jit(solution)/shard_map/pallas_call | solution.py:380
  17.4 1.4 %shard_map.42 = (f32[19,2,16,128]{3,2,1,0:T(8,128)}, f32[3,7,2,16,128]{4,3,2,1,0:T(8,128)}) custom-call(f32[19,2,16,128]{3,2,1,0:T(8,128)S(1)} %get-tuple-element.6.fi, f32[3,7,2,16,128]{4,3,2,1,0:T(8,128)S(1)} %get-tuple-element.7.gi, f32[64,128]{1,0:T(8,128)S(1)} %bitcast.3, f32[2,64,128]{2,1,0:T(8,128)S(1)} %bitcast.2), custom_call_target="tpu_custom_call" | custom-call | tf_op jit(solution)/shard_map/pallas_call | solution.py:404

commit v4 on v3

--- a/solution.py
+++ b/solution.py
@@ -116,7 +116,43 @@
     return out
 
 
-def exchange(sizes, f_hbm, g_hbm, fo, go, ao, yb, fv, gv, q, w, xs, xb, load_sem, send_sem, recv_sem, ready):
+def edge_rows(block, leading, tr, uu, mg):
+    tr[:, 0 : NZ * RX] = block.T
+
+    def turn(p, value):
+        return pltpu.roll(value, VEL[p][0] % NY, 1) if VEL[p][0] else value
+
+    post = collide([turn(p, tr[pl.ds(SLOT[p], 2, stride=64), :]) for p in range(NPOP)])
+    own = 1 if leading == 1 else 0
+    at = {}
+    for p in range(NPOP):
+        if VEL[p][1] == 0:
+            at[p] = SLOT[p]
+            uu[at[p] : at[p] + 1, :] = post[p][own : own + 1]
+        elif VEL[p][1] == leading:
+            at[p] = SLOT[p] - (0 if leading == 1 else 1)
+            uu[at[p] : at[p] + 2, :] = post[p]
+    mg[...] = uu[:, 0 : NZ * RX].T
+    return at
+
+
+def patched(p, z, half, leading, at, mg, value, lane):
+    start = (z ^ zflip(p)) * RX + PAD + 8 * half - VEL[p][0]
+    width = 2 if VEL[p][1] else 1
+    first = 0 if leading == 1 else NY - width
+    patch = pltpu.roll(mg[start : start + 8, :], (first - at[p]) % NY, 1)
+    return jnp.where((lane >= first) & (lane < first + width), patch, value)
+
+
+def near_right(shape):
+    lane = lax.broadcasted_iota(jnp.int32, shape, 1)
+    return (lane < 24) | (((lane < 40) | ((lane >= 88) & (lane < 104))) & (lane % 2 == 0))
+
+
+def exchange(
+    sizes, f_hbm, g_hbm, fo, go, ao, yb, fv, gv, fc, gc, corner, q, w, xs, xb, tr, uu, mg,
+    load_sem, corner_sem, send_sem, recv_sem, ready,
+):
     nx_dev, ny_dev = sizes
     ix, iy = lax.axis_index("gx"), lax.axis_index("gy")
 
@@ -126,6 +162,33 @@
     block = SEAM if ny_dev % SEAM == 0 else ny_dev
     place = lax.rem(iy, block)
     is_first, is_last, is_before = place == 0, place == block - 1, place == block - 2
+
+    barrier = pltpu.get_barrier_semaphore()
+
+    def greet(steps, semaphore):
+        for dx, dy in steps:
+            pl.semaphore_signal(semaphore, inc=1, device_id=device(dx, dy), device_id_type=MESH)
+
+    above = [(-1, 1), (0, 1), (1, 1)]
+
+    @pl.when(is_last)
+    def _():
+        pl.semaphore_wait(barrier, 3)
+        greet([(0, 1)], ready)
+
+    corner_loads = []
+    for z in range(NZ):
+        for side, r in enumerate((0, NX - 2)):
+            to = slice(4 * z + 2 * side, 4 * z + 2 * side + 2)
+            corner_loads += [
+                pltpu.make_async_copy(f_hbm.at[:, z, r : r + 2], fc.at[:, to], corner_sem.at[z, side, 0]),
+                pltpu.make_async_copy(g_hbm.at[:, :, z, r : r + 2], gc.at[:, :, to], corner_sem.at[z, side, 1]),
+            ]
+
+    @pl.when(is_last)
+    def _():
+        for copy in corner_loads:
+            copy.start()
 
     loads = []
     for half in range(2):
@@ -139,21 +202,12 @@
             for copy in piece:
                 copy.start()
 
-    barrier = pltpu.get_barrier_semaphore()
-
-    def greet(steps, semaphore):
-        for dx, dy in steps:
-            pl.semaphore_signal(semaphore, inc=1, device_id=device(dx, dy), device_id_type=MESH)
-
     beside = [(-1, 0), (1, 0)]
-    above = [(-1, 1), (0, 1), (1, 1)]
     below = [(-1, -1), (0, -1), (1, -1)]
 
     @pl.when(is_last)
     def _():
         greet(below, barrier)
-        pl.semaphore_wait(barrier, 3)
-        greet(above, ready)
 
     @pl.when(jnp.logical_not(is_last))
     def _():
@@ -174,15 +228,18 @@
             device_id=device(dx, dy), device_id_type=MESH,
         )
 
-    def to_row(side, dy):
-        return [
-            to(ao.at[:, first], yb.at[side, :, high], -1, dy),
-            to(ao.at[:, last], yb.at[side, :, low], 1, dy),
-            to(ao.at[:, own], yb.at[side, :, own], 0, dy),
-        ]
-
-    to_above = to_row(0, 1)
-    to_below = to_row(1, -1)
+    def to_row(side, dy, dx):
+        if dx == 0:
+            return to(ao.at[:, own], yb.at[side, :, own], 0, dy)
+        src, dst = (slice(8, 10), slice(24, 26)) if dx < 0 else (slice(22, 24), slice(6, 8))
+        return to(ao.at[:, src], yb.at[side, :, dst], dx, dy)
+
+    to_above = [to_row(0, 1, dx) for dx in (-1, 1, 0)]
+    to_below = [to_row(1, -1, dx) for dx in (-1, 1, 0)]
+    with_corners = pltpu.make_async_remote_copy(
+        src_ref=ao.at[:, 6:26], dst_ref=yb.at[1, :, 6:26], send_sem=send_sem.at[5], recv_sem=recv_sem.at[5],
+        device_id=device(0, -1), device_id_type=MESH,
+    )
     to_beside = [
         to(xs.at[0], xb.at[0, :, 0:40], 1, 0),
         to(xs.at[1], xb.at[1, :, 8:48], -1, 0),
@@ -190,9 +247,37 @@
         to(ao.at[:, first], ao.at[:, high], -1, 0),
     ]
 
+    early = [
+        pltpu.make_async_remote_copy(
+            src_ref=corner.at[:, src], dst_ref=yb.at[0, :, dst], send_sem=send_sem.at[k], recv_sem=recv_sem.at[k],
+            device_id=device(dx, 1), device_id_type=MESH,
+        )
+        for k, src, dst, dx in ((0, slice(0, 2), slice(24, 26), -1), (1, slice(2, 4), slice(6, 8), 1))
+    ]
+
     def start(copies):
         for copy in copies:
             copy.start()
+
+    @pl.when(is_last)
+    def _():
+        for copy in corner_loads:
+            copy.wait()
+        pops = [fc[p] for p in range(19)] + [gc[a, j] for a in range(3) for j in range(7)]
+        post = collide(pops)
+        lane = lax.broadcasted_iota(jnp.int32, (8, NY), 1)
+        up = [[jnp.zeros((8, NY), F32) for _ in range(4)] for _ in range(2)]
+        for k, p in enumerate(Y0 + YP):
+            s = SLOT[p]
+            moved = pltpu.roll(post[p], s + 1 + VEL[p][1], 1)
+            here = lane == s if VEL[p][1] == 0 else (lane == s) | (lane == s + 1)
+            up[zflip(p)][k % 4] = jnp.where(here, moved, up[zflip(p)][k % 4])
+        up = [(part[0] + part[1]) + (part[2] + part[3]) for part in up]
+        both = up[0] + pltpu.roll(up[1], 4, 0)
+        both = jnp.where(lane < 64, both, pltpu.roll(both, 63, 1))
+        corner[0] = both[0:4]
+        corner[1] = both[4:8]
+        start(early)
 
     lane = lax.broadcasted_iota(jnp.int32, (8, NY), 1)
     for half in range(2):
@@ -224,12 +309,6 @@
             here = jnp.where((lane < 24) | ((lane < 40) & (lane % 2 == 0)), up[z], down[z])
             there = jnp.where((lane >= 25) & (lane < 40) & (lane % 2 == 1), up[z], down[z])
             ao[z, at, :] = jnp.where(lane < 64, here, pltpu.roll(there, 63, 1))
-        if half == 0:
-
-            @pl.when(is_last)
-            def _():
-                start(to_above[:1])
-
     @pl.when(is_first)
     def _():
         pl.semaphore_wait(barrier, 5)
@@ -244,9 +323,9 @@
 
     @pl.when(jnp.logical_not(is_last))
     def _():
-        start(to_above[:1])
-
-    start(to_above[1:])
+        start(to_above[:2])
+
+    start(to_above[2:])
 
     def row(first, count, z, r):
         return q[pl.ds(first * NZ * RX + z * RX + PAD + r, count, stride=NZ * RX), :]
@@ -308,66 +387,107 @@
                 else:
                     go[(p - 19) // 7, (p - 19) % 7, z, rows, :] = value
 
+    @pl.when(is_last)
+    def _():
+        with_corners.wait_recv()
+
+    @pl.when(jnp.logical_not(is_last))
+    def _():
+        for copy in to_below:
+            copy.wait_recv()
+
+    tall = near_right((NZ * RX, NY))
+    flat = ao[...].reshape(NZ * RX, NY)
+
+    def patch(leading, block):
+        places = edge_rows(block, leading, tr, uu, mg)
+        for p in places:
+            for z in range(NZ):
+                for half in range(2):
+                    rows = slice(8 * half, 8 * half + 8)
+                    if p < 19:
+                        fo[p, z, rows, :] = patched(p, z, half, leading, places, mg, fo[p, z, rows, :], lane)
+                    else:
+                        a, j = (p - 19) // 7, (p - 19) % 7
+                        go[a, j, z, rows, :] = patched(p, z, half, leading, places, mg, go[a, j, z, rows, :], lane)
+
+    patch(-1, jnp.where(tall, flat, yb[1].reshape(NZ * RX, NY)))
+
     @pl.when(is_first)
     def _():
-        pl.semaphore_wait(ready, 3)
-        start(to_below)
-
-    for copy in to_above + to_below:
-        copy.wait()
-
-
-def finish(fi, gi, ao, yb, f_hbm, g_hbm, tr, uu, mg, fo, go, out_sem):
-    lane = lax.broadcasted_iota(jnp.int32, (NZ * RX, NY), 1)
-    near_right = (lane < 24) | (((lane < 40) | ((lane >= 88) & (lane < 104))) & (lane % 2 == 0))
-    tr[0:NY, 0 : NZ * RX] = jnp.where(near_right, yb[0], ao[...]).T
-    tr[NY:, 0 : NZ * RX] = jnp.where(near_right, ao[...], yb[1]).T
-
-    def turn(p, value):
-        return pltpu.roll(value, VEL[p][0] % NY, 1) if VEL[p][0] else value
-
-    post = collide([turn(p, tr[pl.ds(SLOT[p], 4, stride=64), :]) for p in range(NPOP)])
-    shift = {}
-    for p in range(NPOP):
-        if VEL[p][1] == 0:
-            s = 2 * SLOT[p]
-            uu[s : s + 1, :] = post[p][2:3]
-            uu[s + 1 : s + 2, :] = post[p][1:2]
-            shift[p] = NY - 1 - s
-        elif VEL[p][1] == 1:
-            s = 48 + (SLOT[p] - 24)
-            uu[s : s + 2, :] = post[p][0:2]
-            shift[p] = NY - s
-        else:
-            s = 64 + (SLOT[p] - 25)
-            uu[s : s + 2, :] = post[p][2:4]
-            shift[p] = NY - 2 - s
-    mg[...] = uu[:, 0 : NZ * RX].T
+        pl.semaphore_wait(ready, 1)
+        with_corners.start()
+
+    to_above[2].wait_recv()
+    middle = [
+        part
+        for z in range(NZ)
+        for part in (ao[z, low], jnp.where(tall[0:NX], yb[0, z, own], ao[z, own]), ao[z, high])
+    ]
+    patch(1, jnp.concatenate(middle, axis=0))
+
+    @pl.when(is_first)
+    def _():
+        with_corners.wait_send()
+
+    @pl.when(jnp.logical_not(is_first))
+    def _():
+        for copy in to_below:
+            copy.wait_send()
+
+    for copy in to_above:
+        copy.wait_send()
+    for copy in to_above[:2]:
+        copy.wait_recv()
+
+
+def finish(fi, gi, ao, yb, f_hbm, g_hbm, near, post_rows, fo, go, out_sem):
+    mask = near_right((2, NY))
+    for cx in (-1, 0, 1):
+        for z in range(NZ):
+            for k, r in enumerate((-1, NX - 1)):
+                first = z * RX + PAD + r - cx
+                rows = slice(first, first + 2)
+                near[cx % 3, 4 * z + 2 * k : 4 * z + 2 * k + 2, :] = jnp.where(mask, yb[0, rows, :], ao[rows, :])
+    sources = [near[cx] for cx in range(3)]
+    post = collide([pltpu.roll(sources[VEL[p][0] % 3], (64 - SLOT[p]) % NY, 1) for p in range(NPOP)])
     lane = lax.broadcasted_iota(jnp.int32, (8, NY), 1)
-    masks = {0: (lane == 0) | (lane == NY - 1), 1: lane < 2, -1: lane >= NY - 2}
-    stores = [
-        (9, fo.at[0:10], f_hbm.at[0:10]),
-        (18, fo.at[10:19], f_hbm.at[10:19]),
-        (25, go.at[0], g_hbm.at[0]),
-        (32, go.at[1], g_hbm.at[1]),
-        (39, go.at[2], g_hbm.at[2]),
-    ]
+    row = lax.broadcasted_iota(jnp.int32, (8, NY), 0)
+    for p in Y0 + YP:
+        value = post[p]
+        if VEL[p][1]:
+            value = jnp.where(lane == 0, pltpu.roll(value, 64, 1), pltpu.roll(value, 1, 1))
+        post_rows[8 + 8 * p : 16 + 8 * p, :] = value
+
+    def fixed(p, z, half, value):
+        cx, cy, _ = VEL[p]
+        reach = {(0, 0): (0, 1, 1), (1, 0): (7, 1, 2), (0, 1): (0, 2, 0), (1, -1): (6, 2, 2)}.get((half, cx))
+        if cy < 0 or reach is None:
+            return value
+        to, count, at = reach
+        start = 8 + 8 * p + 4 * (z ^ zflip(p)) + at - to
+        here = (row >= to) & (row < to + count) & (lane <= cy)
+        return jnp.where(here, post_rows[start : start + 8, :], value)
+
     copies = []
-    for p in range(NPOP):
-        for z in range(NZ):
-            for half in range(2):
-                start = (z ^ zflip(p)) * RX + PAD + 8 * half - VEL[p][0]
-                patch = pltpu.roll(mg[start : start + 8, :], shift[p], 1)
-                rows = slice(8 * half, 8 * half + 8)
-                if p < 19:
-                    fo[p, z, rows, :] = jnp.where(masks[VEL[p][1]], patch, fi[p, z, rows, :])
-                else:
-                    a, j = (p - 19) // 7, (p - 19) % 7
-                    go[a, j, z, rows, :] = jnp.where(masks[VEL[p][1]], patch, gi[a, j, z, rows, :])
-        for k, (after, src, dst) in enumerate(stores):
-            if after == p:
-                copies.append(pltpu.make_async_copy(src, dst, out_sem.at[k]))
-                copies[-1].start()
+
+    def put(pops, src, dst):
+        for p in pops:
+            for z in range(NZ):
+                for half in range(2):
+                    rows = slice(8 * half, 8 * half + 8)
+                    if p < 19:
+                        fo[p, z, rows, :] = fixed(p, z, half, fi[p, z, rows, :])
+                    else:
+                        a, j = (p - 19) // 7, (p - 19) % 7
+                        go[a, j, z, rows, :] = fixed(p, z, half, gi[a, j, z, rows, :])
+        copies.append(pltpu.make_async_copy(src, dst, out_sem.at[len(copies)]))
+        copies[-1].start()
+
+    put(range(0, 10), fo.at[0:10], f_hbm.at[0:10])
+    put(range(10, 19), fo.at[10:19], f_hbm.at[10:19])
+    put(range(19, 33), go.at[0:2], g_hbm.at[0:2])
+    put(range(33, 40), go.at[2:3], g_hbm.at[2:3])
     for copy in copies:
         copy.wait()
 
@@ -377,6 +497,7 @@
     hbm = pl.BlockSpec(memory_space=pltpu.HBM)
     fluid, magnet = (19, NZ, NX, NY), (3, 7, NZ, NX, NY)
     columns = (NZ, RX, NY)
+    turned = [pltpu.VMEM((NY, NY), F32), pltpu.VMEM((NY, NY), F32), pltpu.VMEM((NZ * RX, NY), F32)]
     fo, go, ao, yb = pl.pallas_call(
         functools.partial(exchange, sizes),
         out_shape=[pltpu.VMEM(shape, F32) for shape in (fluid, magnet, columns, (2, *columns))],
@@ -385,11 +506,16 @@
         scratch_shapes=[
             pltpu.VMEM(fluid, F32),
             pltpu.VMEM(magnet, F32),
+            pltpu.VMEM((19, 8, NY), F32),
+            pltpu.VMEM((3, 7, 8, NY), F32),
+            pltpu.VMEM((NZ, 4, NY), F32),
             pltpu.VMEM((NPOP * NZ * RX, NY), F32),
             pltpu.VMEM((NPOP * NZ * RX, NY), F32),
             pltpu.VMEM((2, NZ, 40, NY), F32),
             pltpu.VMEM((2, NZ, 48, NY), F32),
+            *turned,
             pltpu.SemaphoreType.DMA((2, NZ, 2)),
+            pltpu.SemaphoreType.DMA((NZ, 2, 2)),
             pltpu.SemaphoreType.DMA((10,)),
             pltpu.SemaphoreType.DMA((10,)),
             pltpu.SemaphoreType.REGULAR,
@@ -407,12 +533,11 @@
         in_specs=[vmem] * 4,
         out_specs=[hbm] * 2,
         scratch_shapes=[
-            pltpu.VMEM((2 * NY, NY), F32),
-            pltpu.VMEM((NY, NY), F32),
-            pltpu.VMEM((NZ * RX, NY), F32),
+            pltpu.VMEM((3, 8, NY), F32),
+            pltpu.VMEM((8 * NPOP + 16, NY), F32),
             pltpu.VMEM(fluid, F32),
             pltpu.VMEM(magnet, F32),
-            pltpu.SemaphoreType.DMA((5,)),
+            pltpu.SemaphoreType.DMA((4,)),
         ],
         compiler_params=pltpu.CompilerParams(vmem_limit_bytes=VMEM_LIMIT),
     )(fo, go, ao.reshape(NZ * RX, NY), yb.reshape(2, NZ * RX, NY))

time: 19 us -> 18.4 us (0.968)
  Pallas kernels: 18.2 us -> 17.6 us
    pallas_call x1, Pallas kernels: 1.42 us -> 1.08 us  [per_device(): pl.pallas_call(finish, out_shape=[jax.ShapeDtypeStruct(fluid, F32), jax.S...]
    pallas_call x1, Pallas kernels: 16.8 us -> 16.5 us  [per_device(): pl.pallas_call(functools.partial(exchange, sizes), out_shape=[pltpu.VMEM(...]
where the time goes in v4:
time: 18.4 us; the launch traced here: 18.2 us
  Pallas kernels  17.6 us (96%)
  between operations  0.64 us (3%)
    pallas_call x1, Pallas kernels, per_device(): pl.pallas_call(functools.partial(exchange, sizes), out_shape=[pltpu.VMEM(...  16.5 us
    pallas_call x1, Pallas kernels, per_device(): pl.pallas_call(finish, out_shape=[jax.ShapeDtypeStruct(fluid, F32), jax.S...  1.08 us

profile of v4, /device:TPU:24, one launch (start us, length us, event | category | flops | bytes accessed | tf_op | source)
XLA Modules:
  0.0 18.2 jit_solution(17503449561158099912)
XLA Ops:
  0.6 16.5 %shard_map.41 = (f32[19,2,16,128]{3,2,1,0:T(8,128)S(1)}, f32[3,7,2,16,128]{4,3,2,1,0:T(8,128)S(1)}, f32[2,32,128]{2,1,0:T(8,128)S(1)}, f32[2,2,32,128]{3,2,1,0:T(8,128)S(1)}) custom-call(f32[19,2,16,128]{3,2,1,0:T(8,128)} %f_hbm.1, f32[3,7,2,16,128]{4,3,2,1,0:T(8,128)} %g_hbm.1), custom_call_target="tpu_custom_call" | custom-call | tf_op jit(solution)/shard_map/pallas_call | solution.py:501
  17.2 1.1 %shard_map.42 = (f32[19,2,16,128]{3,2,1,0:T(8,128)}, f32[3,7,2,16,128]{4,3,2,1,0:T(8,128)}) custom-call(f32[19,2,16,128]{3,2,1,0:T(8,128)S(1)} %get-tuple-element.6.fi, f32[3,7,2,16,128]{4,3,2,1,0:T(8,128)S(1)} %get-tuple-element.7.gi, f32[64,128]{1,0:T(8,128)S(1)} %bitcast.3, f32[2,64,128]{2,1,0:T(8,128)S(1)} %bitcast.2), custom_call_target="tpu_custom_call" | custom-call | tf_op jit(solution)/shard_map/pallas_call | solution.py:530

commit v5 on v4

--- a/solution.py
+++ b/solution.py
@@ -150,7 +150,7 @@
 
 
 def exchange(
-    sizes, f_hbm, g_hbm, fo, go, ao, yb, fv, gv, fc, gc, corner, q, w, xs, xb, tr, uu, mg,
+    sizes, f_hbm, g_hbm, fo, go, fe, ge, ao, yb, fv, gv, fc, gc, corner, swap, q, w, xs, xb, tr, uu, mg,
     load_sem, corner_sem, send_sem, recv_sem, ready,
 ):
     nx_dev, ny_dev = sizes
@@ -162,19 +162,6 @@
     block = SEAM if ny_dev % SEAM == 0 else ny_dev
     place = lax.rem(iy, block)
     is_first, is_last, is_before = place == 0, place == block - 1, place == block - 2
-
-    barrier = pltpu.get_barrier_semaphore()
-
-    def greet(steps, semaphore):
-        for dx, dy in steps:
-            pl.semaphore_signal(semaphore, inc=1, device_id=device(dx, dy), device_id_type=MESH)
-
-    above = [(-1, 1), (0, 1), (1, 1)]
-
-    @pl.when(is_last)
-    def _():
-        pl.semaphore_wait(barrier, 3)
-        greet([(0, 1)], ready)
 
     corner_loads = []
     for z in range(NZ):
@@ -189,6 +176,19 @@
     def _():
         for copy in corner_loads:
             copy.start()
+
+    barrier = pltpu.get_barrier_semaphore()
+
+    def greet(steps, semaphore):
+        for dx, dy in steps:
+            pl.semaphore_signal(semaphore, inc=1, device_id=device(dx, dy), device_id_type=MESH)
+
+    above = [(-1, 1), (0, 1), (1, 1)]
+
+    @pl.when(is_last)
+    def _():
+        pl.semaphore_wait(barrier, 3)
+        greet([(0, 1)], ready)
 
     loads = []
     for half in range(2):
@@ -267,16 +267,15 @@
         post = collide(pops)
         lane = lax.broadcasted_iota(jnp.int32, (8, NY), 1)
         up = [[jnp.zeros((8, NY), F32) for _ in range(4)] for _ in range(2)]
-        for k, p in enumerate(Y0 + YP):
-            s = SLOT[p]
-            moved = pltpu.roll(post[p], s + 1 + VEL[p][1], 1)
-            here = lane == s if VEL[p][1] == 0 else (lane == s) | (lane == s + 1)
-            up[zflip(p)][k % 4] = jnp.where(here, moved, up[zflip(p)][k % 4])
+        columns = [(p, SLOT[p], NY - 1 - (1 if VEL[p][1] else 0)) for p in Y0 + YP]
+        columns += [(p, SLOT[p] + 64, NY - 1) for p in YP]
+        for k, (p, s, column) in enumerate(columns):
+            moved = pltpu.roll(post[p], (s - column) % NY, 1)
+            up[zflip(p)][k % 4] = jnp.where(lane == s, moved, up[zflip(p)][k % 4])
         up = [(part[0] + part[1]) + (part[2] + part[3]) for part in up]
-        both = up[0] + pltpu.roll(up[1], 4, 0)
-        both = jnp.where(lane < 64, both, pltpu.roll(both, 63, 1))
-        corner[0] = both[0:4]
-        corner[1] = both[4:8]
+        swap[...] = up[1]
+        corner[0] = up[0][0:4] + swap[4:8, :]
+        corner[1] = up[0][4:8] + swap[0:4, :]
         start(early)
 
     lane = lax.broadcasted_iota(jnp.int32, (8, NY), 1)
@@ -425,6 +424,14 @@
         for part in (ao[z, low], jnp.where(tall[0:NX], yb[0, z, own], ao[z, own]), ao[z, high])
     ]
     patch(1, jnp.concatenate(middle, axis=0))
+    for z in range(NZ):
+        for side, r in enumerate((0, NX - 2)):
+            to = slice(4 * z + 2 * side, 4 * z + 2 * side + 2)
+            for p in range(19):
+                fe[p, to, :] = fo[p, z, r : r + 2, :]
+            for a in range(3):
+                for j in range(7):
+                    ge[a, j, to, :] = go[a, j, z, r : r + 2, :]
 
     @pl.when(is_first)
     def _():
@@ -441,7 +448,16 @@
         copy.wait_recv()
 
 
-def finish(fi, gi, ao, yb, f_hbm, g_hbm, near, post_rows, fo, go, out_sem):
+def finish(fi, gi, fe, ge, ao, yb, f_hbm, g_hbm, near, post_rows, fo, go, out_sem):
+    copies = []
+
+    def store(src, dst):
+        copies.append(pltpu.make_async_copy(src, dst, out_sem.at[len(copies)]))
+        copies[-1].start()
+
+    store(fi.at[:, :, 2 : NX - 2], f_hbm.at[:, :, 2 : NX - 2])
+    store(gi.at[:, :, :, 2 : NX - 2], g_hbm.at[:, :, :, 2 : NX - 2])
+
     mask = near_right((2, NY))
     for cx in (-1, 0, 1):
         for z in range(NZ):
@@ -453,41 +469,35 @@
     post = collide([pltpu.roll(sources[VEL[p][0] % 3], (64 - SLOT[p]) % NY, 1) for p in range(NPOP)])
     lane = lax.broadcasted_iota(jnp.int32, (8, NY), 1)
     row = lax.broadcasted_iota(jnp.int32, (8, NY), 0)
-    for p in Y0 + YP:
-        value = post[p]
-        if VEL[p][1]:
-            value = jnp.where(lane == 0, pltpu.roll(value, 64, 1), pltpu.roll(value, 1, 1))
-        post_rows[8 + 8 * p : 16 + 8 * p, :] = value
-
-    def fixed(p, z, half, value):
+    row = row % 4
+    for p in range(NPOP):
         cx, cy, _ = VEL[p]
-        reach = {(0, 0): (0, 1, 1), (1, 0): (7, 1, 2), (0, 1): (0, 2, 0), (1, -1): (6, 2, 2)}.get((half, cx))
-        if cy < 0 or reach is None:
-            return value
-        to, count, at = reach
-        start = 8 + 8 * p + 4 * (z ^ zflip(p)) + at - to
-        here = (row >= to) & (row < to + count) & (lane <= cy)
-        return jnp.where(here, post_rows[start : start + 8, :], value)
-
-    copies = []
-
-    def put(pops, src, dst):
-        for p in pops:
-            for z in range(NZ):
-                for half in range(2):
-                    rows = slice(8 * half, 8 * half + 8)
-                    if p < 19:
-                        fo[p, z, rows, :] = fixed(p, z, half, fi[p, z, rows, :])
-                    else:
-                        a, j = (p - 19) // 7, (p - 19) % 7
-                        go[a, j, z, rows, :] = fixed(p, z, half, gi[a, j, z, rows, :])
-        copies.append(pltpu.make_async_copy(src, dst, out_sem.at[len(copies)]))
-        copies[-1].start()
-
-    put(range(0, 10), fo.at[0:10], f_hbm.at[0:10])
-    put(range(10, 19), fo.at[10:19], f_hbm.at[10:19])
-    put(range(19, 33), go.at[0:2], g_hbm.at[0:2])
-    put(range(33, 40), go.at[2:3], g_hbm.at[2:3])
+        at = (fe, fo, p) if p < 19 else (ge, go, ((p - 19) // 7, (p - 19) % 7))
+        value = at[0][at[2]]
+        if cy >= 0:
+            new = post[p]
+            if cy:
+                new = jnp.where(lane == 0, pltpu.roll(new, 64, 1), pltpu.roll(new, 1, 1))
+            turned = 4 * zflip(p)
+            if turned or not cx:
+                base = 16 * p
+                post_rows[base : base + 8, :] = new
+                post_rows[base + 8 : base + 16, :] = new
+            if cx:
+                if turned:
+                    new = post_rows[base + turned : base + turned + 8, :]
+                reached = row < 2 if cx > 0 else row >= 2
+                value = jnp.where(reached & (lane <= cy), new, value)
+            else:
+                for shift, reached in ((1, row == 0), (-1, row == 3)):
+                    first = base + (turned + shift) % 8
+                    value = jnp.where(reached & (lane <= cy), post_rows[first : first + 8, :], value)
+        at[1][at[2]] = value
+    for z in range(NZ):
+        for side, r in enumerate((0, NX - 2)):
+            rows = slice(4 * z + 2 * side, 4 * z + 2 * side + 2)
+            store(fo.at[:, rows], f_hbm.at[:, z, r : r + 2])
+            store(go.at[:, :, rows], g_hbm.at[:, :, z, r : r + 2])
     for copy in copies:
         copy.wait()
 
@@ -498,17 +508,19 @@
     fluid, magnet = (19, NZ, NX, NY), (3, 7, NZ, NX, NY)
     columns = (NZ, RX, NY)
     turned = [pltpu.VMEM((NY, NY), F32), pltpu.VMEM((NY, NY), F32), pltpu.VMEM((NZ * RX, NY), F32)]
-    fo, go, ao, yb = pl.pallas_call(
+    edge_f, edge_g = (19, 8, NY), (3, 7, 8, NY)
+    fo, go, fe, ge, ao, yb = pl.pallas_call(
         functools.partial(exchange, sizes),
-        out_shape=[pltpu.VMEM(shape, F32) for shape in (fluid, magnet, columns, (2, *columns))],
+        out_shape=[pltpu.VMEM(shape, F32) for shape in (fluid, magnet, edge_f, edge_g, columns, (2, *columns))],
         in_specs=[hbm] * 2,
-        out_specs=[vmem] * 4,
+        out_specs=[vmem] * 6,
         scratch_shapes=[
             pltpu.VMEM(fluid, F32),
             pltpu.VMEM(magnet, F32),
             pltpu.VMEM((19, 8, NY), F32),
             pltpu.VMEM((3, 7, 8, NY), F32),
             pltpu.VMEM((NZ, 4, NY), F32),
+            pltpu.VMEM((8, NY), F32),
             pltpu.VMEM((NPOP * NZ * RX, NY), F32),
             pltpu.VMEM((NPOP * NZ * RX, NY), F32),
             pltpu.VMEM((2, NZ, 40, NY), F32),
@@ -530,17 +542,17 @@
     return pl.pallas_call(
         finish,
         out_shape=[jax.ShapeDtypeStruct(fluid, F32), jax.ShapeDtypeStruct(magnet, F32)],
-        in_specs=[vmem] * 4,
+        in_specs=[vmem] * 6,
         out_specs=[hbm] * 2,
         scratch_shapes=[
             pltpu.VMEM((3, 8, NY), F32),
-            pltpu.VMEM((8 * NPOP + 16, NY), F32),
-            pltpu.VMEM(fluid, F32),
-            pltpu.VMEM(magnet, F32),
-            pltpu.SemaphoreType.DMA((4,)),
+            pltpu.VMEM((16 * NPOP, NY), F32),
+            pltpu.VMEM(edge_f, F32),
+            pltpu.VMEM(edge_g, F32),
+            pltpu.SemaphoreType.DMA((10,)),
         ],
         compiler_params=pltpu.CompilerParams(vmem_limit_bytes=VMEM_LIMIT),
-    )(fo, go, ao.reshape(NZ * RX, NY), yb.reshape(2, NZ * RX, NY))
+    )(fo, go, fe, ge, ao.reshape(NZ * RX, NY), yb.reshape(2, NZ * RX, NY))
 
 
 VMEM_LIMIT = 48 << 20

time: 18.4 us -> 18.2 us (0.989)
  Pallas kernels: 17.6 us -> 17.4 us
where the time goes in v5:
time: 18.2 us; the launch traced here: 18.1 us
  Pallas kernels  17.4 us (96%)
  between operations  0.64 us (4%)
    pallas_call x1, Pallas kernels, per_device(): pl.pallas_call(functools.partial(exchange, sizes), out_shape=[pltpu.VMEM(...  16.4 us
    pallas_call x1, Pallas kernels, per_device(): pl.pallas_call(finish, out_shape=[jax.ShapeDtypeStruct(fluid, F32), jax.S...  0.97 us

profile of v5, /device:TPU:24, one launch (start us, length us, event | category | flops | bytes accessed | tf_op | source)
XLA Modules:
  0.0 18.1 jit_solution(4036519282209711146)
XLA Ops:
  0.6 16.4 %shard_map.41 = (f32[19,2,16,128]{3,2,1,0:T(8,128)S(1)}, f32[3,7,2,16,128]{4,3,2,1,0:T(8,128)S(1)}, f32[19,8,128]{2,1,0:T(8,128)S(1)}, f32[3,7,8,128]{3,2,1,0:T(...) custom-call(f32[19,2,16,128]{3,2,1,0:T(8,128)} %f_hbm.1, f32[3,7,2,16,128]{4,3,2,1,0:T(8,128)} %g_hbm.1), custom_call_target="tpu_custom_call" | custom-call | tf_op jit(solution)/shard_map/pallas_call | solution.py:512
  17.1 1.0 %shard_map.42 = (f32[19,2,16,128]{3,2,1,0:T(8,128)}, f32[3,7,2,16,128]{4,3,2,1,0:T(8,128)}) custom-call(f32[19,2,16,128]{3,2,1,0:T(8,128)S(1)} %get-tuple-element.8.fi, f32[3,7,2,16,128]{4,3,2,1,0:T(8,128)S(1)} %get-tuple-element.9.gi, f32[19,8,128]{2,1,0:T(8,128)S(1)} %get-tuple-element.10.fe, f32[3,7,8,128]{3,2,1,0:T(8,128)S(1)} %get-tuple-element.11.ge, ...), custom_call_target="tpu_custom_call" | custom-call | tf_op jit(solution)/shard_map/pallas_call | solution.py:542

commit v6 on v5

--- a/solution.py
+++ b/solution.py
@@ -151,7 +151,7 @@
 
 def exchange(
     sizes, f_hbm, g_hbm, fo, go, fe, ge, ao, yb, fv, gv, fc, gc, corner, swap, q, w, xs, xb, tr, uu, mg,
-    load_sem, corner_sem, send_sem, recv_sem, ready,
+    sems, ready,
 ):
     nx_dev, ny_dev = sizes
     ix, iy = lax.axis_index("gx"), lax.axis_index("gy")
@@ -162,14 +162,20 @@
     block = SEAM if ny_dev % SEAM == 0 else ny_dev
     place = lax.rem(iy, block)
     is_first, is_last, is_before = place == 0, place == block - 1, place == block - 2
+
+    corner_loaded, sent, centers_in, corners_in, below_in, beside_in = (sems.at[k] for k in range(6))
+    loaded = [sems.at[6 + half] for half in range(2)]
+
+    def wait(semaphore, rows):
+        pltpu.make_async_copy(q.at[0:rows], q.at[0:rows], semaphore).wait()
 
     corner_loads = []
     for z in range(NZ):
         for side, r in enumerate((0, NX - 2)):
             to = slice(4 * z + 2 * side, 4 * z + 2 * side + 2)
             corner_loads += [
-                pltpu.make_async_copy(f_hbm.at[:, z, r : r + 2], fc.at[:, to], corner_sem.at[z, side, 0]),
-                pltpu.make_async_copy(g_hbm.at[:, :, z, r : r + 2], gc.at[:, :, to], corner_sem.at[z, side, 1]),
+                pltpu.make_async_copy(f_hbm.at[:, z, r : r + 2], fc.at[:, to], corner_loaded),
+                pltpu.make_async_copy(g_hbm.at[:, :, z, r : r + 2], gc.at[:, :, to], corner_loaded),
             ]
 
     @pl.when(is_last)
@@ -190,17 +196,10 @@
         pl.semaphore_wait(barrier, 3)
         greet([(0, 1)], ready)
 
-    loads = []
     for half in range(2):
-        for z in range(NZ):
-            rows = slice(8 * half, 8 * half + 8)
-            piece = (
-                pltpu.make_async_copy(f_hbm.at[:, z, rows], fv.at[:, z, rows], load_sem.at[half, z, 0]),
-                pltpu.make_async_copy(g_hbm.at[:, :, z, rows], gv.at[:, :, z, rows], load_sem.at[half, z, 1]),
-            )
-            loads.append(piece)
-            for copy in piece:
-                copy.start()
+        rows = slice(8 * half, 8 * half + 8)
+        pltpu.make_async_copy(f_hbm.at[:, :, rows], fv.at[:, :, rows], loaded[half]).start()
+        pltpu.make_async_copy(g_hbm.at[:, :, :, rows], gv.at[:, :, :, rows], loaded[half]).start()
 
     beside = [(-1, 0), (1, 0)]
     below = [(-1, -1), (0, -1), (1, -1)]
@@ -219,40 +218,29 @@
 
     low, high, own = slice(0, 8), slice(24, 32), slice(8, 24)
     first, last = slice(8, 16), slice(16, 24)
-    slots = iter(range(10))
-
-    def to(src, dst, dx, dy):
-        k = next(slots)
+
+    def to(src, dst, dx, dy, semaphore):
         return pltpu.make_async_remote_copy(
-            src_ref=src, dst_ref=dst, send_sem=send_sem.at[k], recv_sem=recv_sem.at[k],
+            src_ref=src, dst_ref=dst, send_sem=sent, recv_sem=semaphore,
             device_id=device(dx, dy), device_id_type=MESH,
         )
 
-    def to_row(side, dy, dx):
-        if dx == 0:
-            return to(ao.at[:, own], yb.at[side, :, own], 0, dy)
-        src, dst = (slice(8, 10), slice(24, 26)) if dx < 0 else (slice(22, 24), slice(6, 8))
-        return to(ao.at[:, src], yb.at[side, :, dst], dx, dy)
-
-    to_above = [to_row(0, 1, dx) for dx in (-1, 1, 0)]
-    to_below = [to_row(1, -1, dx) for dx in (-1, 1, 0)]
-    with_corners = pltpu.make_async_remote_copy(
-        src_ref=ao.at[:, 6:26], dst_ref=yb.at[1, :, 6:26], send_sem=send_sem.at[5], recv_sem=recv_sem.at[5],
-        device_id=device(0, -1), device_id_type=MESH,
-    )
+    def corners(block, side, dy, semaphore, lo, hi):
+        return [
+            to(block.at[:, lo : lo + 2], yb.at[side, :, 24:26], -1, dy, semaphore),
+            to(block.at[:, hi : hi + 2], yb.at[side, :, 6:8], 1, dy, semaphore),
+        ]
+
+    early = corners(corner, 0, 1, corners_in, 0, 2)
+    above_corners = corners(ao, 0, 1, corners_in, 8, 22)
+    above_center = to(ao.at[:, own], yb.at[0, :, own], 0, 1, centers_in)
+    to_below = corners(ao, 1, -1, below_in, 8, 22) + [to(ao.at[:, own], yb.at[1, :, own], 0, -1, below_in)]
+    with_corners = to(ao.at[:, 6:26], yb.at[1, :, 6:26], 0, -1, below_in)
     to_beside = [
-        to(xs.at[0], xb.at[0, :, 0:40], 1, 0),
-        to(xs.at[1], xb.at[1, :, 8:48], -1, 0),
-        to(ao.at[:, last], ao.at[:, low], 1, 0),
-        to(ao.at[:, first], ao.at[:, high], -1, 0),
-    ]
-
-    early = [
-        pltpu.make_async_remote_copy(
-            src_ref=corner.at[:, src], dst_ref=yb.at[0, :, dst], send_sem=send_sem.at[k], recv_sem=recv_sem.at[k],
-            device_id=device(dx, 1), device_id_type=MESH,
-        )
-        for k, src, dst, dx in ((0, slice(0, 2), slice(24, 26), -1), (1, slice(2, 4), slice(6, 8), 1))
+        to(xs.at[0], xb.at[0, :, 0:40], 1, 0, beside_in),
+        to(xs.at[1], xb.at[1, :, 8:48], -1, 0, beside_in),
+        to(ao.at[:, last], ao.at[:, low], 1, 0, beside_in),
+        to(ao.at[:, first], ao.at[:, high], -1, 0, beside_in),
     ]
 
     def start(copies):
@@ -261,8 +249,7 @@
 
     @pl.when(is_last)
     def _():
-        for copy in corner_loads:
-            copy.wait()
+        wait(corner_loaded, 8 * NPOP)
         pops = [fc[p] for p in range(19)] + [gc[a, j] for a in range(3) for j in range(7)]
         post = collide(pops)
         lane = lax.broadcasted_iota(jnp.int32, (8, NY), 1)
@@ -284,9 +271,8 @@
         at = slice(PAD + 8 * half, PAD + 8 * half + 8)
         up = [jnp.zeros((8, NY), F32) for _ in range(NZ)]
         down = [jnp.zeros((8, NY), F32) for _ in range(NZ)]
+        wait(loaded[half], 8 * NZ * NPOP)
         for z in range(NZ):
-            for copy in loads[half * NZ + z]:
-                copy.wait()
             pops = [fv[p, z, rows, :] for p in range(19)]
             pops += [gv[a, j, z, rows, :] for a in range(3) for j in range(7)]
             post = collide(pops)
@@ -322,9 +308,9 @@
 
     @pl.when(jnp.logical_not(is_last))
     def _():
-        start(to_above[:2])
-
-    start(to_above[2:])
+        start(above_corners)
+
+    above_center.start()
 
     def row(first, count, z, r):
         return q[pl.ds(first * NZ * RX + z * RX + PAD + r, count, stride=NZ * RX), :]
@@ -349,8 +335,7 @@
     def _():
         start(to_below)
 
-    for copy in to_beside:
-        copy.wait()
+    wait(beside_in, 2 * NZ * 48)
 
     def turn(p, value):
         return pltpu.roll(value, VEL[p][1] % NY, 1) if VEL[p][1] else value
@@ -386,15 +371,7 @@
                 else:
                     go[(p - 19) // 7, (p - 19) % 7, z, rows, :] = value
 
-    @pl.when(is_last)
-    def _():
-        with_corners.wait_recv()
-
-    @pl.when(jnp.logical_not(is_last))
-    def _():
-        for copy in to_below:
-            copy.wait_recv()
-
+    wait(below_in, NZ * 20)
     tall = near_right((NZ * RX, NY))
     flat = ao[...].reshape(NZ * RX, NY)
 
@@ -417,7 +394,7 @@
         pl.semaphore_wait(ready, 1)
         with_corners.start()
 
-    to_above[2].wait_recv()
+    wait(centers_in, NZ * NX)
     middle = [
         part
         for z in range(NZ)
@@ -433,30 +410,14 @@
                 for j in range(7):
                     ge[a, j, to, :] = go[a, j, z, r : r + 2, :]
 
-    @pl.when(is_first)
-    def _():
-        with_corners.wait_send()
-
-    @pl.when(jnp.logical_not(is_first))
-    def _():
-        for copy in to_below:
-            copy.wait_send()
-
-    for copy in to_above:
-        copy.wait_send()
-    for copy in to_above[:2]:
-        copy.wait_recv()
+    wait(sent, NZ * (20 + 20) + 2 * NZ * 48)
+    wait(corners_in, NZ * 4)
 
 
 def finish(fi, gi, fe, ge, ao, yb, f_hbm, g_hbm, near, post_rows, fo, go, out_sem):
-    copies = []
-
-    def store(src, dst):
-        copies.append(pltpu.make_async_copy(src, dst, out_sem.at[len(copies)]))
-        copies[-1].start()
-
-    store(fi.at[:, :, 2 : NX - 2], f_hbm.at[:, :, 2 : NX - 2])
-    store(gi.at[:, :, :, 2 : NX - 2], g_hbm.at[:, :, :, 2 : NX - 2])
+    stored_f, stored_g = out_sem.at[0], out_sem.at[1]
+    pltpu.make_async_copy(fi.at[:, :, 2 : NX - 2], f_hbm.at[:, :, 2 : NX - 2], stored_f).start()
+    pltpu.make_async_copy(gi.at[:, :, :, 2 : NX - 2], g_hbm.at[:, :, :, 2 : NX - 2], stored_g).start()
 
     mask = near_right((2, NY))
     for cx in (-1, 0, 1):
@@ -496,10 +457,10 @@
     for z in range(NZ):
         for side, r in enumerate((0, NX - 2)):
             rows = slice(4 * z + 2 * side, 4 * z + 2 * side + 2)
-            store(fo.at[:, rows], f_hbm.at[:, z, r : r + 2])
-            store(go.at[:, :, rows], g_hbm.at[:, :, z, r : r + 2])
-    for copy in copies:
-        copy.wait()
+            pltpu.make_async_copy(fo.at[:, rows], f_hbm.at[:, z, r : r + 2], stored_f).start()
+            pltpu.make_async_copy(go.at[:, :, rows], g_hbm.at[:, :, z, r : r + 2], stored_g).start()
+    pltpu.make_async_copy(fi, f_hbm, stored_f).wait()
+    pltpu.make_async_copy(gi, g_hbm, stored_g).wait()
 
 
 def per_device(sizes, fluid_pops, magnet_pops):
@@ -526,10 +487,7 @@
             pltpu.VMEM((2, NZ, 40, NY), F32),
             pltpu.VMEM((2, NZ, 48, NY), F32),
             *turned,
-            pltpu.SemaphoreType.DMA((2, NZ, 2)),
-            pltpu.SemaphoreType.DMA((NZ, 2, 2)),
-            pltpu.SemaphoreType.DMA((10,)),
-            pltpu.SemaphoreType.DMA((10,)),
+            pltpu.SemaphoreType.DMA((8,)),
             pltpu.SemaphoreType.REGULAR,
         ],
         compiler_params=pltpu.CompilerParams(
@@ -549,7 +507,7 @@
             pltpu.VMEM((16 * NPOP, NY), F32),
             pltpu.VMEM(edge_f, F32),
             pltpu.VMEM(edge_g, F32),
-            pltpu.SemaphoreType.DMA((10,)),
+            pltpu.SemaphoreType.DMA((2,)),
         ],
         compiler_params=pltpu.CompilerParams(vmem_limit_bytes=VMEM_LIMIT),
     )(fo, go, fe, ge, ao.reshape(NZ * RX, NY), yb.reshape(2, NZ * RX, NY))

time: 18.2 us -> 17.9 us (0.984)
  Pallas kernels: 17.4 us -> 17.1 us
    pallas_call x1, Pallas kernels: 16.4 us -> 16.2 us  [per_device(): pl.pallas_call(functools.partial(exchange, sizes), out_shape=[pltpu.VMEM(...]
where the time goes in v6:
time: 17.9 us; the launch traced here: 17.7 us
  Pallas kernels  17.1 us (96%)
  between operations  0.64 us (4%)
    pallas_call x1, Pallas kernels, per_device(): pl.pallas_call(functools.partial(exchange, sizes), out_shape=[pltpu.VMEM(...  16.2 us
    pallas_call x1, Pallas kernels, per_device(): pl.pallas_call(finish, out_shape=[jax.ShapeDtypeStruct(fluid, F32), jax.S...  0.9 us

profile of v6, /device:TPU:24, one launch (start us, length us, event | category | flops | bytes accessed | tf_op | source)
XLA Modules:
  0.0 17.7 jit_solution(17665806392423224281)
XLA Ops:
  0.6 16.2 %shard_map.41 = (f32[19,2,16,128]{3,2,1,0:T(8,128)S(1)}, f32[3,7,2,16,128]{4,3,2,1,0:T(8,128)S(1)}, f32[19,8,128]{2,1,0:T(8,128)S(1)}, f32[3,7,8,128]{3,2,1,0:T(...) custom-call(f32[19,2,16,128]{3,2,1,0:T(8,128)} %f_hbm.1, f32[3,7,2,16,128]{4,3,2,1,0:T(8,128)} %g_hbm.1), custom_call_target="tpu_custom_call" | custom-call | tf_op jit(solution)/shard_map/pallas_call | solution.py:473
  16.8 0.9 %shard_map.42 = (f32[19,2,16,128]{3,2,1,0:T(8,128)}, f32[3,7,2,16,128]{4,3,2,1,0:T(8,128)}) custom-call(f32[19,2,16,128]{3,2,1,0:T(8,128)S(1)} %get-tuple-element.8.fi, f32[3,7,2,16,128]{4,3,2,1,0:T(8,128)S(1)} %get-tuple-element.9.gi, f32[19,8,128]{2,1,0:T(8,128)S(1)} %get-tuple-element.10.fe, f32[3,7,8,128]{3,2,1,0:T(8,128)S(1)} %get-tuple-element.11.ge, ...), custom_call_target="tpu_custom_call" | custom-call | tf_op jit(solution)/shard_map/pallas_call | solution.py:500

commit v7 on v6

--- a/solution.py
+++ b/solution.py
@@ -71,8 +71,7 @@
         for value, sign in terms[1:]:
             total = total + value if sign > 0 else total - value
         mom.append(total)
-    inv = 1.0 / rho
-    u = [m * inv for m in mom]
+    u = [m / rho for m in mom]
     b = [((g[a][0] + g[a][1]) + (g[a][2] + g[a][3])) + ((g[a][4] + g[a][5]) + g[a][6]) for a in range(3)]
     half = 0.5 * (b[0] * b[0] + b[1] * b[1] + b[2] * b[2])
     diag = [mom[a] * u[a] - b[a] * b[a] + half for a in range(3)]
@@ -117,7 +116,7 @@
 
 
 def edge_rows(block, leading, tr, uu, mg):
-    tr[:, 0 : NZ * RX] = block.T
+    tr[0:NY, 0 : NZ * RX] = block.T
 
     def turn(p, value):
         return pltpu.roll(value, VEL[p][0] % NY, 1) if VEL[p][0] else value
@@ -150,7 +149,7 @@
 
 
 def exchange(
-    sizes, f_hbm, g_hbm, fo, go, fe, ge, ao, yb, fv, gv, fc, gc, corner, swap, q, w, xs, xb, tr, uu, mg,
+    sizes, f_hbm, g_hbm, fo, go, fe, ge, ao, yb, fv, gv, fc, gc, corner, q, w, xs, xb, tr, uu, mg,
     sems, ready,
 ):
     nx_dev, ny_dev = sizes
@@ -163,25 +162,18 @@
     place = lax.rem(iy, block)
     is_first, is_last, is_before = place == 0, place == block - 1, place == block - 2
 
-    corner_loaded, sent, centers_in, corners_in, below_in, beside_in = (sems.at[k] for k in range(6))
-    loaded = [sems.at[6 + half] for half in range(2)]
+    sent, centers_in, corners_in, below_in, beside_in = (sems.at[k] for k in range(5))
+    loaded = [sems.at[5 + half] for half in range(2)]
+    corner_loaded = [sems.at[7 + side] for side in range(2)]
 
     def wait(semaphore, rows):
         pltpu.make_async_copy(q.at[0:rows], q.at[0:rows], semaphore).wait()
 
-    corner_loads = []
-    for z in range(NZ):
+    @pl.when(is_last)
+    def _():
         for side, r in enumerate((0, NX - 2)):
-            to = slice(4 * z + 2 * side, 4 * z + 2 * side + 2)
-            corner_loads += [
-                pltpu.make_async_copy(f_hbm.at[:, z, r : r + 2], fc.at[:, to], corner_loaded),
-                pltpu.make_async_copy(g_hbm.at[:, :, z, r : r + 2], gc.at[:, :, to], corner_loaded),
-            ]
-
-    @pl.when(is_last)
-    def _():
-        for copy in corner_loads:
-            copy.start()
+            pltpu.make_async_copy(f_hbm.at[:, :, r : r + 2], fc.at[side], corner_loaded[side]).start()
+            pltpu.make_async_copy(g_hbm.at[:, :, :, r : r + 2], gc.at[side], corner_loaded[side]).start()
 
     barrier = pltpu.get_barrier_semaphore()
 
@@ -231,7 +223,10 @@
             to(block.at[:, hi : hi + 2], yb.at[side, :, 6:8], 1, dy, semaphore),
         ]
 
-    early = corners(corner, 0, 1, corners_in, 0, 2)
+    early = [
+        to(corner.at[0], yb.at[0, :, 24:26], -1, 1, corners_in),
+        to(corner.at[1], yb.at[0, :, 6:8], 1, 1, corners_in),
+    ]
     above_corners = corners(ao, 0, 1, corners_in, 8, 22)
     above_center = to(ao.at[:, own], yb.at[0, :, own], 0, 1, centers_in)
     to_below = corners(ao, 1, -1, below_in, 8, 22) + [to(ao.at[:, own], yb.at[1, :, own], 0, -1, below_in)]
@@ -249,21 +244,21 @@
 
     @pl.when(is_last)
     def _():
-        wait(corner_loaded, 8 * NPOP)
-        pops = [fc[p] for p in range(19)] + [gc[a, j] for a in range(3) for j in range(7)]
-        post = collide(pops)
-        lane = lax.broadcasted_iota(jnp.int32, (8, NY), 1)
-        up = [[jnp.zeros((8, NY), F32) for _ in range(4)] for _ in range(2)]
+        lane = lax.broadcasted_iota(jnp.int32, (2, NY), 1)
         columns = [(p, SLOT[p], NY - 1 - (1 if VEL[p][1] else 0)) for p in Y0 + YP]
         columns += [(p, SLOT[p] + 64, NY - 1) for p in YP]
-        for k, (p, s, column) in enumerate(columns):
-            moved = pltpu.roll(post[p], (s - column) % NY, 1)
-            up[zflip(p)][k % 4] = jnp.where(lane == s, moved, up[zflip(p)][k % 4])
-        up = [(part[0] + part[1]) + (part[2] + part[3]) for part in up]
-        swap[...] = up[1]
-        corner[0] = up[0][0:4] + swap[4:8, :]
-        corner[1] = up[0][4:8] + swap[0:4, :]
-        start(early)
+        for side in range(2):
+            wait(corner_loaded[side], 2 * NZ * NPOP)
+            up = [[jnp.zeros((2, NY), F32) for _ in range(4)] for _ in range(NZ)]
+            for z in range(NZ):
+                pops = [fc[side, p, z] for p in range(19)] + [gc[side, a, j, z] for a in range(3) for j in range(7)]
+                post = collide(pops)
+                for k, (p, s, column) in enumerate(columns):
+                    part = up[z ^ zflip(p)]
+                    part[k % 4] = jnp.where(lane == s, pltpu.roll(post[p], (s - column) % NY, 1), part[k % 4])
+            for z in range(NZ):
+                corner[side, z] = (up[z][0] + up[z][1]) + (up[z][2] + up[z][3])
+            early[side].start()
 
     lane = lax.broadcasted_iota(jnp.int32, (8, NY), 1)
     for half in range(2):
@@ -468,7 +463,7 @@
     hbm = pl.BlockSpec(memory_space=pltpu.HBM)
     fluid, magnet = (19, NZ, NX, NY), (3, 7, NZ, NX, NY)
     columns = (NZ, RX, NY)
-    turned = [pltpu.VMEM((NY, NY), F32), pltpu.VMEM((NY, NY), F32), pltpu.VMEM((NZ * RX, NY), F32)]
+    turned = [pltpu.VMEM((NY + 64, NY), F32), pltpu.VMEM((NY, NY), F32), pltpu.VMEM((NZ * RX, NY), F32)]
     edge_f, edge_g = (19, 8, NY), (3, 7, 8, NY)
     fo, go, fe, ge, ao, yb = pl.pallas_call(
         functools.partial(exchange, sizes),
@@ -478,16 +473,15 @@
         scratch_shapes=[
             pltpu.VMEM(fluid, F32),
             pltpu.VMEM(magnet, F32),
-            pltpu.VMEM((19, 8, NY), F32),
-            pltpu.VMEM((3, 7, 8, NY), F32),
-            pltpu.VMEM((NZ, 4, NY), F32),
-            pltpu.VMEM((8, NY), F32),
-            pltpu.VMEM((NPOP * NZ * RX, NY), F32),
+            pltpu.VMEM((2, 19, NZ, 2, NY), F32),
+            pltpu.VMEM((2, 3, 7, NZ, 2, NY), F32),
+            pltpu.VMEM((2, NZ, 2, NY), F32),
+            pltpu.VMEM(((NPOP + 1) * NZ * RX, NY), F32),
             pltpu.VMEM((NPOP * NZ * RX, NY), F32),
             pltpu.VMEM((2, NZ, 40, NY), F32),
             pltpu.VMEM((2, NZ, 48, NY), F32),
             *turned,
-            pltpu.SemaphoreType.DMA((8,)),
+            pltpu.SemaphoreType.DMA((9,)),
             pltpu.SemaphoreType.REGULAR,
         ],
         compiler_params=pltpu.CompilerParams(

time: 17.9 us -> 17.9 us (level)
  no operation moved by 1% of the time
where the time goes in v7:
time: 17.9 us; the launch traced here: 17.7 us
  Pallas kernels  17.1 us (96%)
  between operations  0.64 us (4%)
    pallas_call x1, Pallas kernels, per_device(): pl.pallas_call(functools.partial(exchange, sizes), out_shape=[pltpu.VMEM(...  16.2 us
    pallas_call x1, Pallas kernels, per_device(): pl.pallas_call(finish, out_shape=[jax.ShapeDtypeStruct(fluid, F32), jax.S...  0.9 us

profile of v7, /device:TPU:24, one launch (start us, length us, event | category | flops | bytes accessed | tf_op | source)
XLA Modules:
  0.0 17.7 jit_solution(5383840014937581602)
XLA Ops:
  0.6 16.2 %shard_map.41 = (f32[19,2,16,128]{3,2,1,0:T(8,128)S(1)}, f32[3,7,2,16,128]{4,3,2,1,0:T(8,128)S(1)}, f32[19,8,128]{2,1,0:T(8,128)S(1)}, f32[3,7,8,128]{3,2,1,0:T(...) custom-call(f32[19,2,16,128]{3,2,1,0:T(8,128)} %f_hbm.1, f32[3,7,2,16,128]{4,3,2,1,0:T(8,128)} %g_hbm.1), custom_call_target="tpu_custom_call" | custom-call | tf_op jit(solution)/shard_map/pallas_call | solution.py:468
  16.8 0.9 %shard_map.42 = (f32[19,2,16,128]{3,2,1,0:T(8,128)}, f32[3,7,2,16,128]{4,3,2,1,0:T(8,128)}) custom-call(f32[19,2,16,128]{3,2,1,0:T(8,128)S(1)} %get-tuple-element.8.fi, f32[3,7,2,16,128]{4,3,2,1,0:T(8,128)S(1)} %get-tuple-element.9.gi, f32[19,8,128]{2,1,0:T(8,128)S(1)} %get-tuple-element.10.fe, f32[3,7,8,128]{3,2,1,0:T(8,128)S(1)} %get-tuple-element.11.ge, ...), custom_call_target="tpu_custom_call" | custom-call | tf_op jit(solution)/shard_map/pallas_call | solution.py:494

commit v8 on v7

--- a/solution.py
+++ b/solution.py
@@ -426,7 +426,12 @@
     lane = lax.broadcasted_iota(jnp.int32, (8, NY), 1)
     row = lax.broadcasted_iota(jnp.int32, (8, NY), 0)
     row = row % 4
-    for p in range(NPOP):
+    strips = [
+        (z, r, slice(4 * z + 2 * side, 4 * z + 2 * side + 2))
+        for z in range(NZ)
+        for side, r in enumerate((0, NX - 2))
+    ]
+    for p in [*range(19, NPOP), *range(19)]:
         cx, cy, _ = VEL[p]
         at = (fe, fo, p) if p < 19 else (ge, go, ((p - 19) // 7, (p - 19) % 7))
         value = at[0][at[2]]
@@ -449,11 +454,11 @@
                     first = base + (turned + shift) % 8
                     value = jnp.where(reached & (lane <= cy), post_rows[first : first + 8, :], value)
         at[1][at[2]] = value
-    for z in range(NZ):
-        for side, r in enumerate((0, NX - 2)):
-            rows = slice(4 * z + 2 * side, 4 * z + 2 * side + 2)
-            pltpu.make_async_copy(fo.at[:, rows], f_hbm.at[:, z, r : r + 2], stored_f).start()
-            pltpu.make_async_copy(go.at[:, :, rows], g_hbm.at[:, :, z, r : r + 2], stored_g).start()
+        if p == 39:
+            for z, r, rows in strips:
+                pltpu.make_async_copy(go.at[:, :, rows], g_hbm.at[:, :, z, r : r + 2], stored_g).start()
+    for z, r, rows in strips:
+        pltpu.make_async_copy(fo.at[:, rows], f_hbm.at[:, z, r : r + 2], stored_f).start()
     pltpu.make_async_copy(fi, f_hbm, stored_f).wait()
     pltpu.make_async_copy(gi, g_hbm, stored_g).wait()
 

time: 17.9 us -> 17.9 us (level)
  no operation moved by 1% of the time
where the time goes in v8:
time: 17.9 us; the launch traced here: 17.7 us
  Pallas kernels  17.1 us (96%)
  between operations  0.64 us (4%)
    pallas_call x1, Pallas kernels, per_device(): pl.pallas_call(functools.partial(exchange, sizes), out_shape=[pltpu.VMEM(...  16.2 us
    pallas_call x1, Pallas kernels, per_device(): pl.pallas_call(finish, out_shape=[jax.ShapeDtypeStruct(fluid, F32), jax.S...  0.89 us

profile of v8, /device:TPU:24, one launch (start us, length us, event | category | flops | bytes accessed | tf_op | source)
XLA Modules:
  0.0 17.7 jit_solution(16341776706430689030)
XLA Ops:
  0.6 16.2 %shard_map.41 = (f32[19,2,16,128]{3,2,1,0:T(8,128)S(1)}, f32[3,7,2,16,128]{4,3,2,1,0:T(8,128)S(1)}, f32[19,8,128]{2,1,0:T(8,128)S(1)}, f32[3,7,8,128]{3,2,1,0:T(...) custom-call(f32[19,2,16,128]{3,2,1,0:T(8,128)} %f_hbm.1, f32[3,7,2,16,128]{4,3,2,1,0:T(8,128)} %g_hbm.1), custom_call_target="tpu_custom_call" | custom-call | tf_op jit(solution)/shard_map/pallas_call | solution.py:473
  16.8 0.9 %shard_map.42 = (f32[19,2,16,128]{3,2,1,0:T(8,128)}, f32[3,7,2,16,128]{4,3,2,1,0:T(8,128)}) custom-call(f32[19,2,16,128]{3,2,1,0:T(8,128)S(1)} %get-tuple-element.8.fi, f32[3,7,2,16,128]{4,3,2,1,0:T(8,128)S(1)} %get-tuple-element.9.gi, f32[19,8,128]{2,1,0:T(8,128)S(1)} %get-tuple-element.10.fe, f32[3,7,8,128]{3,2,1,0:T(8,128)S(1)} %get-tuple-element.11.ge, ...), custom_call_target="tpu_custom_call" | custom-call | tf_op jit(solution)/shard_map/pallas_call | solution.py:499

commit v9 on v8

--- a/solution.py
+++ b/solution.py
@@ -162,9 +162,9 @@
     place = lax.rem(iy, block)
     is_first, is_last, is_before = place == 0, place == block - 1, place == block - 2
 
-    sent, centers_in, corners_in, below_in, beside_in = (sems.at[k] for k in range(5))
-    loaded = [sems.at[5 + half] for half in range(2)]
-    corner_loaded = [sems.at[7 + side] for side in range(2)]
+    sent, centers_in, corners_in, others_in = (sems.at[k] for k in range(4))
+    loaded = [sems.at[4 + half] for half in range(2)]
+    corner_loaded = [sems.at[6 + side] for side in range(2)]
 
     def wait(semaphore, rows):
         pltpu.make_async_copy(q.at[0:rows], q.at[0:rows], semaphore).wait()
@@ -229,13 +229,13 @@
     ]
     above_corners = corners(ao, 0, 1, corners_in, 8, 22)
     above_center = to(ao.at[:, own], yb.at[0, :, own], 0, 1, centers_in)
-    to_below = corners(ao, 1, -1, below_in, 8, 22) + [to(ao.at[:, own], yb.at[1, :, own], 0, -1, below_in)]
-    with_corners = to(ao.at[:, 6:26], yb.at[1, :, 6:26], 0, -1, below_in)
+    to_below = corners(ao, 1, -1, others_in, 8, 22) + [to(ao.at[:, own], yb.at[1, :, own], 0, -1, others_in)]
+    with_corners = to(ao.at[:, 6:26], yb.at[1, :, 6:26], 0, -1, others_in)
     to_beside = [
-        to(xs.at[0], xb.at[0, :, 0:40], 1, 0, beside_in),
-        to(xs.at[1], xb.at[1, :, 8:48], -1, 0, beside_in),
-        to(ao.at[:, last], ao.at[:, low], 1, 0, beside_in),
-        to(ao.at[:, first], ao.at[:, high], -1, 0, beside_in),
+        to(xs.at[0], xb.at[0, :, 0:40], 1, 0, others_in),
+        to(xs.at[1], xb.at[1, :, 8:48], -1, 0, others_in),
+        to(ao.at[:, last], ao.at[:, low], 1, 0, others_in),
+        to(ao.at[:, first], ao.at[:, high], -1, 0, others_in),
     ]
 
     def start(copies):
@@ -330,7 +330,7 @@
     def _():
         start(to_below)
 
-    wait(beside_in, 2 * NZ * 48)
+    wait(others_in, 2 * NZ * 48 + NZ * 20)
 
     def turn(p, value):
         return pltpu.roll(value, VEL[p][1] % NY, 1) if VEL[p][1] else value
@@ -366,7 +366,6 @@
                 else:
                     go[(p - 19) // 7, (p - 19) % 7, z, rows, :] = value
 
-    wait(below_in, NZ * 20)
     tall = near_right((NZ * RX, NY))
     flat = ao[...].reshape(NZ * RX, NY)
 
@@ -486,7 +485,7 @@
             pltpu.VMEM((2, NZ, 40, NY), F32),
             pltpu.VMEM((2, NZ, 48, NY), F32),
             *turned,
-            pltpu.SemaphoreType.DMA((9,)),
+            pltpu.SemaphoreType.DMA((8,)),
             pltpu.SemaphoreType.REGULAR,
         ],
         compiler_params=pltpu.CompilerParams(

time: 17.9 us -> 17.9 us (level)
  no operation moved by 1% of the time
where the time goes in v9:
time: 17.9 us; the launch traced here: 17.7 us
  Pallas kernels  17.1 us (96%)
  between operations  0.64 us (4%)
    pallas_call x1, Pallas kernels, per_device(): pl.pallas_call(functools.partial(exchange, sizes), out_shape=[pltpu.VMEM(...  16.2 us
    pallas_call x1, Pallas kernels, per_device(): pl.pallas_call(finish, out_shape=[jax.ShapeDtypeStruct(fluid, F32), jax.S...  0.89 us

profile of v9, /device:TPU:24, one launch (start us, length us, event | category | flops | bytes accessed | tf_op | source)
XLA Modules:
  0.0 17.7 jit_solution(1925589421869664338)
XLA Ops:
  0.6 16.2 %shard_map.41 = (f32[19,2,16,128]{3,2,1,0:T(8,128)S(1)}, f32[3,7,2,16,128]{4,3,2,1,0:T(8,128)S(1)}, f32[19,8,128]{2,1,0:T(8,128)S(1)}, f32[3,7,8,128]{3,2,1,0:T(...) custom-call(f32[19,2,16,128]{3,2,1,0:T(8,128)} %f_hbm.1, f32[3,7,2,16,128]{4,3,2,1,0:T(8,128)} %g_hbm.1), custom_call_target="tpu_custom_call" | custom-call | tf_op jit(solution)/shard_map/pallas_call | solution.py:472
  16.8 0.9 %shard_map.42 = (f32[19,2,16,128]{3,2,1,0:T(8,128)}, f32[3,7,2,16,128]{4,3,2,1,0:T(8,128)}) custom-call(f32[19,2,16,128]{3,2,1,0:T(8,128)S(1)} %get-tuple-element.8.fi, f32[3,7,2,16,128]{4,3,2,1,0:T(8,128)S(1)} %get-tuple-element.9.gi, f32[19,8,128]{2,1,0:T(8,128)S(1)} %get-tuple-element.10.fe, f32[3,7,8,128]{3,2,1,0:T(8,128)S(1)} %get-tuple-element.11.ge, ...), custom_call_target="tpu_custom_call" | custom-call | tf_op jit(solution)/shard_map/pallas_call | solution.py:498
